TPU v7x, 256 devices: a whole 4x4x8 slice. The times are simulated.
256 devices in a mesh: cfg: 2 (over core), seq: 32 (over z_hi, y, x), head: 4 (over z_lo).
Axes of the slice: x: 4, y: 4, z: 8 (z_hi: 2, z_lo: 4; z = z_hi * 4 + z_lo), core: 2. Of those that a mesh axis runs over, the one named last changes fastest.
Arguments:
- latent: bfloat16 [32768, 1152], P('seq')
- modulation: float32 [2, 6, 1152], P('cfg'), may hold values from -3 to 3
- w_qkv_space: bfloat16 [1152, 3, 1152], P(None, None, 'head')
- w_out_space: bfloat16 [1152, 1152], P('head'), may hold values from -0.1875 to 0.1875
- w_qkv_time: bfloat16 [1152, 3, 1152], P(None, None, 'head')
- w_out_time: bfloat16 [1152, 1152], P('head'), may hold values from -0.1875 to 0.1875
- clip_frames: int32 [4], replicated, may hold values from 1 to 32, 64 in all
- spatial_window: int32 [512], replicated, may hold values from 0 to 14, as said below
Outputs:
- guided: bfloat16 [32768, 1152], P('seq', 'cfg')
Inputs may be any that keep to these rules, and one draw needn't show every extreme that they name: `clip_frames`: positive, summing to 64, the largest exactly 32. `spatial_window`: positions form 512 // 16 rows of 16; tiles of 8 x 8 are laid after an offset of 1 to 7 rows and 1 to 7 columns, so edge tiles are cut; row r, column c has number ((r + offset rows) // 8) * 3 + (c + offset columns) // 8; every number in the range occurs.
All inputs are finite; a program needn't handle non-finite values.
Results may differ from a plain program's by a relative error of at most 0.02.
Values may be sent and summed in bfloat16 or wider, within the bound.
A program may use at most 64 MiB of HBM per device.

v0:
```python
import jax
import jax.numpy as jnp
from jax import lax
from jax.sharding import PartitionSpec as P

HEAD_DIM = 72
POSITIONS = 512
CLIPS = 4


GUIDE = 4.0
EPSILON = 1e-06


def from_partner(value, axis, apart):
    mask = 2**apart
    pairs = [(source, source ^ mask) for source in range(lax.axis_size(axis))]
    return lax.ppermute(value, axis, pairs)


def modulate(token_rows, shift_vec, scale_vec):
    values = token_rows.astype(jnp.float32)
    centre = jnp.mean(values, axis=-1, keepdims=True)
    centered = values - centre
    spread = jnp.mean(centered * centered, axis=-1, keepdims=True)
    normed = centered * lax.rsqrt(spread + EPSILON)
    return (normed * (1.0 + shift_vec * 0.0 + scale_vec) + shift_vec).astype(jnp.bfloat16)


def softmax_weights(scores, allowed):
    scores = jnp.where(allowed, scores, -1e30)
    row_top = jnp.max(scores, axis=-1, keepdims=True)
    expo_terms = jnp.exp(scores - row_top)
    return (expo_terms / jnp.sum(expo_terms, axis=-1, keepdims=True)).astype(jnp.bfloat16)


def window_mask(clip_frames, all_frames, window_len):
    clip_ends = jnp.cumsum(clip_frames)
    clip_starts = clip_ends - clip_frames
    frame_ids = jnp.arange(all_frames, dtype=jnp.int32)
    clip_of = jnp.sum((frame_ids[:, None] >= clip_ends[None, :]).astype(jnp.int32), axis=1)
    clip_ids = jnp.arange(CLIPS, dtype=jnp.int32)
    start_of = jnp.sum(
        jnp.where(clip_of[:, None] == clip_ids[None, :], clip_starts[None, :], 0), axis=1
    )
    window = clip_of * all_frames + (frame_ids - start_of) // window_len
    return window[:, None] == window[None, :]


def shards(
    latent,
    modulation,
    w_qkv_space,
    w_out_space,
    w_qkv_time,
    w_out_time,
    clip_frames,
    spatial_window,
):
    rows_dev, width = latent.shape
    groups = lax.axis_size("seq")
    head_cols = w_qkv_space.shape[2]
    local_heads = head_cols // HEAD_DIM
    frame_dev = rows_dev // POSITIONS
    all_frames = frame_dev * groups
    slab_rows = POSITIONS // groups
    factors = modulation[0]
    scaling = HEAD_DIM ** (-0.5)
    modded = modulate(latent, factors[0], factors[1])
    packed = jnp.dot(
        modded, w_qkv_space.reshape(width, 3 * head_cols), preferred_element_type=jnp.float32
    ).astype(jnp.bfloat16)
    packed = packed.reshape(frame_dev, POSITIONS, 3, local_heads, HEAD_DIM)
    scores = (
        jnp.einsum(
            "fqhd,fkhd->fhqk", packed[:, :, 0], packed[:, :, 1], preferred_element_type=jnp.float32
        )
        * scaling
    )
    same_window = spatial_window[:, None] == spatial_window[None, :]
    weights = softmax_weights(scores, same_window)
    attended = jnp.einsum(
        "fhqk,fkhd->fqhd", weights, packed[:, :, 2], preferred_element_type=jnp.float32
    ).astype(jnp.bfloat16)
    partial_value = jnp.dot(
        attended.reshape(rows_dev, head_cols), w_out_space, preferred_element_type=jnp.float32
    )
    same_span = window_mask(clip_frames, all_frames, all_frames // 4)
    projected = lax.psum(partial_value, "head").astype(jnp.bfloat16)
    after_space = (latent.astype(jnp.float32) + factors[2] * projected.astype(jnp.float32)).astype(
        jnp.bfloat16
    )
    columns = after_space.reshape(frame_dev, groups, slab_rows, width)
    piece = lax.all_to_all(columns, "seq", split_axis=1, concat_axis=0, tiled=True)
    number_items = piece.shape[2]
    token_rows = piece.reshape(all_frames, number_items, width)
    modded_time = modulate(token_rows, factors[3], factors[4])
    packed_time = jnp.dot(
        modded_time.reshape(all_frames * number_items, width),
        w_qkv_time.reshape(width, 3 * head_cols),
        preferred_element_type=jnp.float32,
    ).astype(jnp.bfloat16)
    packed_time = packed_time.reshape(all_frames, number_items, 3, local_heads, HEAD_DIM)
    scores_time = (
        jnp.einsum(
            "fphd,gphd->phfg",
            packed_time[:, :, 0],
            packed_time[:, :, 1],
            preferred_element_type=jnp.float32,
        )
        * scaling
    )
    weights_time = softmax_weights(scores_time, same_span)
    attended_time = jnp.einsum(
        "phfg,gphd->fphd", weights_time, packed_time[:, :, 2], preferred_element_type=jnp.float32
    ).astype(jnp.bfloat16)
    attended_time = attended_time.reshape(all_frames, number_items, head_cols)
    partial_time = jnp.dot(
        attended_time.reshape(all_frames * number_items, head_cols),
        w_out_time,
        preferred_element_type=jnp.float32,
    )
    summed = lax.psum(partial_time.astype(jnp.bfloat16), "head")
    result = summed.reshape(all_frames, number_items, width)
    moved_width = result.shape[2]
    returned = lax.all_to_all(
        result.reshape(groups, frame_dev, slab_rows, moved_width),
        "seq",
        split_axis=0,
        concat_axis=2,
        tiled=True,
    )
    returned = returned.reshape(rows_dev, moved_width)
    after_time = (
        after_space.astype(jnp.float32) + factors[5] * returned.astype(jnp.float32)
    ).astype(jnp.bfloat16)
    branch = lax.axis_index("cfg")
    half_cols = width // 2
    other_rows = from_partner(after_time, "cfg", 0)
    own_half = lax.dynamic_slice_in_dim(after_time, branch * half_cols, half_cols, 1)
    theirs = lax.dynamic_slice_in_dim(other_rows, branch * half_cols, half_cols, 1)
    cond_half = jnp.where(branch == 0, own_half, theirs)
    uncond = jnp.where(branch == 0, theirs, own_half)
    uncond_vals = uncond.astype(jnp.float32)
    return (uncond_vals + GUIDE * (cond_half.astype(jnp.float32) - uncond_vals)).astype(
        jnp.bfloat16
    )


def solution(mesh):
    return jax.shard_map(
        shards,
        mesh=mesh,
        in_specs=(
            P("seq", None),
            P("cfg", None, None),
            P(None, None, "head"),
            P("head", None),
            P(None, None, "head"),
            P("head", None),
            P(),
            P(),
        ),
        out_specs=P("seq", "cfg"),
        check_vma=False,
    )
```

profile of v0, /device:TPU:6, one launch (start us, length us, event | category | flops | bytes accessed | tf_op | source)
XLA Modules:
  0.0 490.1 jit_solution(4231712165235149429)
XLA Ops:
  6.5 1.6 slice_reduce_fusion
  8.1 2.0 convert_reduce_fusion
  10.2 0.8 fusion.5
  11.0 3.9 fusion.33
  14.9 4.5 reshape.198
  19.4 1.5 fusion.53
  20.9 0.2 broadcast_compare_fusion
  21.1 5.5 %fusion.54 = (f32[2,4,512]{2,1,0:T(4,128)S(1)}, f32[2,4,512,512]{2,3,1,0:T(8,128)}) fusion(pred[512,512]{0,1:T(8,128)(4,1)S(1)} %broadcast_compare_fusion, bf16[2,512,1,4,72]{1,0,4,3,2:T(2,128)(2,1)S(1)} %get-tuple-element.15, bf16[2,512,1,4,72]{1,0,4,3,2:T(2,128)(2,1)S(1)} %get-tuple-element.16), kind=kOutput, calls=%fused_computation.95 | convolution fusion | flops 310379008 | bytes 9846784 | tf_op jit(solution)/shard_map/sub | solution.py:33
  26.6 4.2 fusion.38
  30.8 0.0 copy-start.7
  30.9 0.6 copy.51
  31.5 0.1 copy.69
  31.6 0.4 copy-done.7
  31.9 3.6 fusion.56
  35.6 166.0 %all-reduce.4 = bf16[1024,1152]{1,0:T(8,128)(2,1)} all-reduce(f32[1024,1152]{1,0:T(8,128)} %fusion.56), channel_id=1, replica_groups=mesh['cfg'=2,'seq'=32,'head'=4] {'head'}, use_global_device_ids=true, to_apply=%region_4.5 | all-reduce | flops 1179648 | bytes 7077888 | tf_op jit(solution)/shard_map/psum | solution.py:89
  201.5 2.4 fusion.9
  203.9 1.4 copy-done.4
  205.3 1.6 copy.52
  206.9 11.0 %all-to-all-start = ((bf16[2,32,16,1152]{3,2,0,1:T(8,128)(2,1)}), bf16[2,32,16,1152]{3,2,0,1:T(8,128)(2,1)S(1)}, u32[]{:S(2)}, u32[]{:S(2)}) async-start(bf16[2,32,16,1152]{3,2,0,1:T(8,128)(2,1)} %copy.52), calls=%async_computation | async-start | bytes 4718592 | tf_op jit(solution)/shard_map/all_to_all | solution.py:94
  217.9 0.0 all-reduce.3.cloned.1.call-start
  218.0 0.2 reduce-window.8
  218.2 0.1 convert_reduce_fusion.1
  218.2 0.1 select_reduce_fusion
  218.4 0.1 broadcast_compare_fusion.1
  218.4 37.8 %all-to-all-done = bf16[2,32,16,1152]{3,2,0,1:T(8,128)(2,1)S(1)} async-done(((bf16[2,32,16,1152]{3,2,0,1:T(8,128)(2,1)}), bf16[2,32,16,1152]{3,2,0,1:T(8,128)(2,1)S(1)}, u32[]{:S(2)}, u32[]{:S(2)}) %all-to-all-start) | async-done | bytes 2359328 | tf_op jit(solution)/shard_map/all_to_all | solution.py:94
  256.2 0.4 fusion.13
  256.6 0.8 fusion.16
  257.4 0.9 fusion.19
  258.4 0.6 copy-done.11
  259.0 2.5 convolution_convert_fusion.1
  261.5 2.5 copy.53
  263.9 5.6 %reshape.202 = bf16[64,16,3,4,72]{4,3,2,1,0:T(4,128)(2,1)S(1)} reshape(bf16[1024,864]{1,0:T(8,128)(2,1)} %copy.53) | data formatting | bytes 3538944 | tf_op jit(solution)/shard_map/reshape | solution.py:103
  269.6 3.0 fusion.52
  272.6 3.6 fusion.55
  276.2 1.3 fusion.36
  277.5 0.8 copy.58
  278.3 0.7 reshape_reshape.6
  279.0 2.9 convolution_convert_fusion
  281.9 0.0 all-reduce.3.cloned.1.call-update
  281.9 119.1 %all-reduce.3.cloned.1.call-done = bf16[32,2,16,1152]{3,2,1,0:T(8,128)(2,1)} async-done(((bf16[32,2,16,1152]{3,2,1,0:T(8,128)(2,1)}), bf16[32,2,16,1152]{3,2,1,0:T(8,128)(2,1)}) %all-reduce.3.cloned.1.call-update) | async-done | bytes 2359312 | tf_op jit(solution)/shard_map/psum | solution.py:123
  401.0 68.2 %all_to_all.8 = bf16[32,2,16,1152]{3,2,1,0:T(8,128)(2,1)S(1)} all-to-all(bf16[32,2,16,1152]{3,2,1,0:T(8,128)(2,1)} %all-reduce.3.cloned.1.call-done), channel_id=1, replica_groups=mesh['cfg'=2,'seq'=32,'head'=4] {'seq'}, dimensions={0} | all-to-all | bytes 4718592 | tf_op jit(solution)/shard_map/all_to_all | solution.py:126
  469.2 0.6 convert_bitcast_fusion
  469.8 0.4 copy.59
  470.2 1.3 copy-done.5
  471.4 2.0 fusion.11
  473.5 4.9 collective-permute-done
  478.3 3.5 fusion.25
  481.8 1.4 copy.60
  (31 shorter events, 0.1 us)
Async XLA Ops:
  6.5 4.5 copy-start
  6.5 3.7 copy-start.2
  19.4 1.5 copy-start.10
  30.8 1.1 copy-start.7
  35.6 166.0 %copy-start.3 = (bf16[1024,1152]{1,0:T(8,128)(2,1)S(1)}, bf16[1024,1152]{1,0:T(8,128)(2,1)}, u32[]{:S(2)}) copy-start(bf16[1024,1152]{1,0:T(8,128)(2,1)} %param.8) | copy-start | bytes 7077892
  35.6 166.0 %copy-start.9 = (f32[1152]{0:T(1024)S(1)}, f32[1152]{0:T(1024)}, u32[]{:S(2)}) copy-start(f32[1152]{0:T(1024)} %get-tuple-element.8) | copy-start | bytes 13828
  203.9 1.4 copy-start.4
  206.9 11.0 %copy-start.13 = (s32[4]{0:T(128)S(1)}, s32[4]{0:T(128)}, u32[]{:S(2)}) copy-start(s32[4]{0:T(128)} %param.14) | copy-start | bytes 52
  206.9 49.3 %all-to-all-start = ((bf16[2,32,16,1152]{3,2,0,1:T(8,128)(2,1)}), bf16[2,32,16,1152]{3,2,0,1:T(8,128)(2,1)S(1)}, u32[]{:S(2)}, u32[]{:S(2)}) async-start(bf16[2,32,16,1152]{3,2,0,1:T(8,128)(2,1)} %copy.52), calls=%async_computation | async-start | bytes 4718592 | tf_op jit(solution)/shard_map/all_to_all | solution.py:94
  217.9 183.1 %all-reduce.3.cloned.1.call-start = ((), (), s32[]{:S(2)}) async-start(), calls=%async_computation.2 | async-start | bytes 4718592 | tf_op jit(solution)/shard_map/psum | solution.py:123
  257.4 1.6 copy-start.11
  272.6 3.6 copy-start.6
  277.5 1.5 copy-start.12
  469.8 1.7 copy-start.5
  469.8 1.7 copy-start.8
  473.5 4.9 collective-permute-start
  473.5 9.8 %copy-start.1 = (bf16[1152,3,288]{0,2,1:T(8,128)(2,1)S(1)}, bf16[1152,3,288]{0,2,1:T(8,128)(2,1)}, u32[]{:S(2)}) copy-start(bf16[1152,3,288]{0,2,1:T(8,128)(2,1)} %param.10) | copy-start | bytes 5971972
Sparse Core Ops, SparseCore 0:
  282.0 118.9 all-reduce.2
where the time goes:
time: 492 us; the launch traced here: 490 us
  blocking collectives  234 us (48%)
  waiting for transfers between devices  162 us (33%)
  matrix products  27.5 us (6%)
  local copies, waits for them, and re-layouts  26.3 us (5%)
  other arithmetic  15.7 us (3%)
  between operations  13.7 us (3%)
  starting transfers between devices  11 us (2%)
    psum x1, blocking collectives, shards(): projected = lax.psum(partial_value, 'head').astype(jnp.bfloat16)  166 us
    psum x1, waiting for transfers between devices, shards(): summed = lax.psum(partial_time.astype(jnp.bfloat16), 'head')  119 us
    all_to_all x1, blocking collectives, shards(): lax.all_to_all(result.reshape(groups, frame_dev, slab_rows, moved_width),...  68.2 us
    all_to_all x1, waiting for transfers between devices, shards(): lax.all_to_all(columns, 'seq', split_axis=1, concat_axis=0, tiled=True)  37.8 us
    all_to_all x1, starting transfers between devices, shards(): lax.all_to_all(columns, 'seq', split_axis=1, concat_axis=0, tiled=True)  11 us
  transfers between devices with their start and end apart: 3, of which 3 were waited for; matrix products, arithmetic and copies ran while one was open for 0% of the time, Pallas kernels for 0%

commit v1 on v0

v1 whole, which is shorter than its diff:
```python
import functools

import jax
import jax.numpy as jnp
from jax import lax
from jax.experimental import pallas as pl
from jax.experimental.pallas import tpu as pltpu
from jax.sharding import PartitionSpec as P

MESH = pl.DeviceIdType.MESH
HEAD_DIM = 72
POSITIONS = 512
WIDTH = 1152
HALF = 576
LOCAL = 288
PAIR = 144
TWIN = 16
GUIDE = 4.0
EPSILON = 1e-06
NEG = -1e30
PAD = 128
RING = 8
PLANE = 16
GROUP = 16
EXP_SCALE = HEAD_DIM ** (-0.5) * 1.4426950408889634
BF = jnp.bfloat16
F32 = jnp.float32


def iota(shape, dim):
    return lax.broadcasted_iota(jnp.int32, shape, dim)


def modulated(rows, shift, scale):
    values = rows.astype(F32)
    centred = values - jnp.mean(values, axis=-1, keepdims=True)
    spread = jnp.mean(centred * centred, axis=-1, keepdims=True)
    normed = centred * lax.rsqrt(spread + EPSILON)
    return (normed * (1.0 + scale) + shift).astype(BF)


def softmax(scores):
    top = jnp.max(scores, axis=-1, keepdims=True)
    terms = jnp.exp2((scores - top) * EXP_SCALE)
    return (terms * (1.0 / jnp.sum(terms, axis=-1, keepdims=True))).astype(BF)


def dot(a, b):
    return lax.dot_general(a, b, (((1,), (0,)), ((), ())), preferred_element_type=F32)


def dot_t(a, b):
    return lax.dot_general(a, b, (((1,), (1,)), ((), ())), preferred_element_type=F32)


def head_mask(head, lanes):
    lane = iota((1, lanes), 1)
    return jnp.where((lane >= head * HEAD_DIM) & (lane < (head + 1) * HEAD_DIM), 1.0, 0.0)


def frame_window(frame, clip_ref):
    ends = [clip_ref[0]]
    for j in range(1, 4):
        ends.append(ends[-1] + clip_ref[j])
    clip = jnp.zeros_like(frame)
    start = jnp.zeros_like(frame)
    for end in ends:
        clip = clip + jnp.where(frame >= end, 1, 0)
        start = jnp.where(frame >= end, end, start)
    return clip * 64 + (frame - start) // TWIN


def kernel(
    sw_ref, clip_ref, lat, mod, wsp, wo, wt, out,
    modx, xb, qs, ks, vs, base, att, heads, wos, lats, xs, xt, wbuf, tbias, xn, os_, psend, precv, gs, g2, gz,
    mod_s, lat_s, wo_s, wo_r, wz_s, wz_r, wp_s, wp_r, za_s, za_r, xy_s, xy_r, sb_s, sb_r, pp_s, r1_s, r1_r, r2_s, r2_r,
):
    c = lax.axis_index("cfg")
    s = lax.axis_index("seq")
    h = lax.axis_index("head")
    zh = s // PLANE
    i = s % PLANE
    y = i // 4
    x = i % 4
    z = zh * 4 + h

    def on_z(zz):
        return (c, (zz // 4) * PLANE + i, zz % 4)

    def on_plane(ii):
        return (c, zh * PLANE + ii, h)

    sib = (1 - c, s, h)

    def remote(src, dst, send, recv, dev):
        return pltpu.make_async_remote_copy(
            src_ref=src, dst_ref=dst, send_sem=send, recv_sem=recv, device_id=dev, device_id_type=MESH
        )

    def landed(buf, recv):
        remote(buf, buf, recv, recv, sib).wait_recv()

    def sent(buf, send):
        remote(buf, buf, send, send, sib).wait_send()

    barrier = pltpu.get_barrier_semaphore()

    def greet_z(k, _):
        pl.semaphore_signal(barrier, inc=1, device_id=on_z((z + k) % RING), device_id_type=MESH)
        return 0

    def greet_plane(k, _):
        pl.semaphore_signal(barrier, inc=1, device_id=on_plane((i + k) % PLANE), device_id_type=MESH)
        return 0

    lax.fori_loop(1, RING, greet_z, 0)
    lax.fori_loop(1, PLANE, greet_plane, 0)
    pl.semaphore_signal(barrier, inc=1, device_id=sib, device_id_type=MESH)
    pl.semaphore_wait(barrier, RING - 1 + PLANE - 1 + 1)

    far = jnp.where(c == 0, 2, RING - 2)

    def shard_rows(j):
        return (i + 12 * j) % GROUP

    def weight_piece(j, t):
        first = shard_rows(j)
        flat = 36 * j + first + 16 * t
        return first + 16 * t, flat // 16

    hops = [RING - 1, far, 1]
    for j in range(3):
        for t in range(3):
            row, q = weight_piece(j, t)
            copy = remote(
                wt.at[pl.ds(row * GROUP, GROUP)], wbuf.at[q, y, x], wz_s.at[j, t], wz_r.at[j, t], on_z((z + hops[j]) % RING)
            )
            if t < 2:
                copy.start()
            else:
                pl.when(row < 36)(copy.start)

    mod_copy = remote(mod, modx, mod_s.at[0], mod_s.at[1], sib)
    mod_copy.start()
    lat_out = remote(
        lat.at[c, pl.ds(64 * (7 - z), 64)], lats.at[zh * 2 + c], lat_s.at[0], lat_s.at[1], on_z(7 - z)
    )
    lat_out.start()
    wo_rows = pl.ds(PAIR * c, PAIR)
    for k, hop in enumerate([1, RING - 1, far]):
        remote(wo.at[wo_rows], wos.at[h, wo_rows], wo_s.at[k], wo_r.at[k], on_z((z + hop) % RING)).start()

    oy = jnp.int32(7)
    ox = jnp.int32(7)
    for r in range(1, 8):
        oy = oy - jnp.where(sw_ref[16 * r] < 3, 1, 0)
        ox = ox - jnp.where(sw_ref[r] < 1, 1, 0)
    qj = iota((128, 384), 0)
    ki = iota((128, 384), 1)
    same = ((qj // 16 + 8 + oy) // 8 == (ki // 16 + oy) // 8) & ((qj % 16 + ox) // 8 == (ki % 16 + ox) // 8)
    base[...] = jnp.where(same, 0.0, NEG)

    def time_key(row):
        four = row % 4
        frame = (four // 2) * 32 + 2 * (row // 16) + four % 2
        return frame_window(frame, clip_ref) * 4 + (row % 16) // 4

    tbias[...] = jnp.where(time_key(iota((256, 1), 0)) == time_key(iota((1, 256), 1)), 0.0, NEG)

    for ref in (ks, vs):
        ref[0:PAD, :] = jnp.zeros((PAD, 384), BF)
        ref[PAD + POSITIONS :, :] = jnp.zeros((PAD, 384), BF)
        ref[PAD : PAD + POSITIONS, 256:384] = jnp.zeros((POSITIONS, 128), BF)
    qs[:, 256:384] = jnp.zeros((POSITIONS, 128), BF)

    shift1, scale1 = mod[0:1, :], mod[1:2, :]
    masks = [head_mask(n, 384) for n in range(4)]

    for f in range(2):

        def project(rb, _):
            rows = pl.ds(rb * 256, 256)
            values = modulated(lat[f, rows, :], shift1, scale1)
            qs[rows, 0:LOCAL] = dot(values, wsp[0]).astype(BF)
            ks[pl.ds(PAD + rb * 256, 256), 0:LOCAL] = dot(values, wsp[1]).astype(BF)
            vs[pl.ds(PAD + rb * 256, 256), 0:LOCAL] = dot(values, wsp[2]).astype(BF)
            return 0

        lax.fori_loop(0, 2, project, 0)

        def attend(k, _):
            query = qs[pl.ds(k * 128, 128), :]
            stacked = jnp.concatenate([query * m.astype(BF) for m in masks], axis=0)
            keys = ks[pl.ds(k * 128, 384), :]
            vals = vs[pl.ds(k * 128, 384), :]
            row = 8 * k - 8 + iota((1, 384), 1) // 16
            bias = base[...] + jnp.where((row >= 0) & (row < 32), 0.0, NEG)
            scores = dot_t(stacked, keys) + jnp.concatenate([bias] * 4, axis=0)
            mixed = dot(softmax(scores), vals)
            total = mixed[0:128] * masks[0]
            for n in range(1, 4):
                total = total + mixed[128 * n : 128 * (n + 1)] * masks[n]
            att[f, pl.ds(k * 128, 128), :] = total.astype(BF)
            for t in range(2):
                zd = 2 * k + t
                block = att.at[f, pl.ds(64 * zd, 64)]
                copy = remote(block, heads.at[h, zh * 2 + f], za_s.at[f, zd], za_r.at[f, z], on_z(zd))
                pl.when(zd != z)(copy.start)

                @pl.when(zd == z)
                def _():
                    heads[h, zh * 2 + f] = att[f, pl.ds(64 * zd, 64), :]

            return 0

        lax.fori_loop(0, 4, attend, 0)

        if f == 0:
            for j in range(3):
                for t in range(3):
                    row, q = weight_piece(j, t)
                    wait = functools.partial(landed, wbuf.at[q, y, x], wz_r.at[j, t])
                    if t < 2:
                        wait()
                    else:
                        pl.when(row < 36)(wait)
            for k in range(1, 4):
                to_x = (x + k) % 4
                to_y = (y + k) % 4
                piece = wbuf.at[0:4, y, x]
                remote(piece, piece, wp_s.at[0, k], wp_r.at[0, k], on_plane(4 * y + to_x)).start()
                piece = wbuf.at[4:7, y, x]
                remote(piece, piece, wp_s.at[1, k], wp_r.at[1, k], on_plane(4 * to_y + x)).start()
            piece = lats.at[(1 - zh) * 2 + c]
            landed(piece, lat_s.at[1])
            remote(piece, piece, lat_s.at[2], lat_s.at[3], sib).start()

    for k in range(1, 4):
        from_x = (x + 4 - k) % 4
        from_y = (y + 4 - k) % 4
        landed(wbuf.at[0:4, y, from_x], wp_r.at[0, k])
        landed(wbuf.at[4:7, from_y, x], wp_r.at[1, k])
    for k in range(1, 4):
        to_x = (x + k) % 4
        to_y = (y + k) % 4
        piece = wbuf.at[0:4, y]
        remote(piece, piece, wp_s.at[2, k], wp_r.at[2, k], on_plane(4 * to_y + x)).start()
        piece = wbuf.at[4:7, :, x]
        remote(piece, piece, wp_s.at[3, k], wp_r.at[3, k], on_plane(4 * y + to_x)).start()

    for k, hop in enumerate([RING - 1, 1, 2]):
        piece = wos.at[(h + hop) % 4, wo_rows]
        landed(piece, wo_r.at[k])
        remote(piece, piece, wo_s.at[3 + k], wo_r.at[3 + k], sib).start()
    wos[h] = wo[...]
    lats[pl.ds(zh * 2, 2)] = lat[:, pl.ds(64 * z, 64), :]
    landed(lats.at[(1 - zh) * 2 + (1 - c)], lat_s.at[3])
    for k, hop in enumerate([RING - 1, 1, 2]):
        landed(wos.at[(h + hop) % 4, pl.ds(PAIR * (1 - c), PAIR)], wo_r.at[3 + k])

    def take_heads(k, _):
        zz = (z + k) % RING
        for f in range(2):
            landed(heads.at[zz % 4, (zz // 4) * 2 + f], za_r.at[f, zz])
        return 0

    lax.fori_loop(1, RING, take_heads, 0)

    gate1 = mod[2:3, :]
    order = jnp.where(iota((256, 256), 1) == (iota((256, 256), 0) % 4) * 64 + iota((256, 256), 0) // 4, 1.0, 0.0).astype(BF)
    for n in range(3):
        cols = slice(384 * n, 384 * (n + 1))
        total = jnp.zeros((256, 384), F32)
        for g in range(4):
            total = total + dot(heads[g].reshape(256, 384)[:, 0:LOCAL], wos[g, :, cols])
        after = lats[:, :, cols].reshape(256, 384).astype(F32) + gate1[:, cols] * total.astype(BF).astype(F32)
        xs[:, :, cols] = dot(order, after.astype(BF)).astype(BF).reshape(PLANE, 16, 384)

    def give(k, _):
        to = (i + k) % PLANE
        remote(xs.at[to], xt.at[0, i], xy_s.at[to], xy_r.at[i], on_plane(to)).start()
        return 0

    lax.fori_loop(1, PLANE, give, 0)
    xt[0, i] = xs[i]
    remote(xs.at[i], xt.at[1, i], sb_s.at[i], sb_r.at[i], sib).start()

    def pass_on(k, _):
        source = (i + PLANE - k) % PLANE
        piece = xt.at[0, source]
        landed(piece, xy_r.at[source])
        remote(piece, xt.at[1, source], sb_s.at[source], sb_r.at[source], sib).start()
        return 0

    lax.fori_loop(1, PLANE, pass_on, 0)
    xn[0:256, :] = modulated(xt[0].reshape(256, WIDTH), mod[3:4, :], mod[4:5, :])

    def take_sibling(k, _):
        landed(xt.at[1, k], sb_r.at[k])
        return 0

    lax.fori_loop(0, PLANE, take_sibling, 0)
    mod_copy.wait()
    xn[256:512, :] = modulated(xt[1].reshape(256, WIDTH), modx[3:4, :], modx[4:5, :])

    for k in range(1, 4):
        from_x = (x + 4 - k) % 4
        from_y = (y + 4 - k) % 4
        landed(wbuf.at[0:4, from_y], wp_r.at[2, k])
        landed(wbuf.at[4:7, :, from_x], wp_r.at[3, k])

    def weight_rows(slot, first, count):
        if slot == 0:
            return wt[first * 16 : (first + count) * 16, :]
        flat = 36 * (slot - 1) + first
        return jnp.concatenate([wbuf[p // 16, (p % 16) // 4, p % 4] for p in range(flat, flat + count)], axis=0)

    pair_masks = [head_mask(n, PAIR) for n in range(2)]
    for slot in range(4):
        values = xn[...]
        query = dot_t(values, weight_rows(slot, 0, 9)).astype(BF)
        keys = dot_t(values, weight_rows(slot, 9, 9)).astype(BF)
        vals = dot_t(values, weight_rows(slot, 18, 9)).astype(BF)
        for b in range(2):
            rows = slice(256 * b, 256 * (b + 1))
            stacked = jnp.concatenate([query[rows] * m.astype(BF) for m in pair_masks], axis=0)
            scores = dot_t(stacked, keys[rows]) + jnp.concatenate([tbias[...]] * 2, axis=0)
            mixed = dot(softmax(scores), vals[rows])
            os_[slot, rows, :] = (mixed[0:256] * pair_masks[0] + mixed[256:512] * pair_masks[1]).astype(BF)

    def share(first):
        total = jnp.zeros((512, 640), F32)
        for slot in range(4):
            if slot == 0:
                weights = wt[27 * 16 : 36 * 16, pl.ds(first, 640)]
            else:
                flat = 36 * (slot - 1) + 27
                weights = jnp.concatenate(
                    [wbuf[p // 16, (p % 16) // 4, p % 4, :, pl.ds(first, 640)] for p in range(flat, flat + 9)], axis=0
                )
            total = total + dot(os_[slot], weights)
        return total

    theirs = pl.multiple_of(512 * (1 - c), 128)
    mine = pl.multiple_of(512 * c, 128)
    psend[...] = share(theirs).astype(BF)
    give_share = remote(psend, precv, pp_s.at[0], pp_s.at[1], sib)
    give_share.start()
    own = share(mine)
    give_share.wait()
    results = []
    for b in range(2):
        gate = (mod if b == 0 else modx)[5:6, pl.ds(mine, 640)]
        other = precv[256 * (1 - b) : 256 * (2 - b), :]
        total = (own[256 * b : 256 * (b + 1)] + other.astype(F32)).astype(BF).astype(F32)
        before = xt[b, :, :, pl.ds(mine, 640)].reshape(256, 640).astype(F32)
        results.append((before + gate * total).astype(BF).astype(F32))
    cond = jnp.where(c == 0, results[0], results[1])
    uncond = jnp.where(c == 0, results[1], results[0])
    guided = (uncond + GUIDE * (cond - uncond)).astype(BF)
    guided = jnp.where(c == 0, guided[:, 0:HALF], guided[:, 64 : 64 + HALF])
    gs[...] = guided.reshape(PLANE, 16, HALF)

    def back(k, _):
        to = (i + k) % PLANE
        remote(gs.at[to], g2.at[i], r1_s.at[to], r1_r.at[i], on_plane(to)).start()
        return 0

    lax.fori_loop(1, PLANE, back, 0)
    g2[i] = gs[i]

    def take_back(k, _):
        source = (i + PLANE - k) % PLANE
        landed(g2.at[source], r1_r.at[source])
        return 0

    lax.fori_loop(1, PLANE, take_back, 0)
    order = jnp.where(iota((256, 256), 1) == (iota((256, 256), 0) % 64) * 4 + iota((256, 256), 0) // 64, 1.0, 0.0).astype(BF)
    gz[...] = dot(order, g2[...].reshape(256, HALF)).astype(BF).reshape(4, 64, HALF)

    def spread(k, _):
        zd = (z + k) % RING
        place = out.at[:, pl.ds(64 * z, 64)]
        remote(gz.at[pl.ds((zd // 4) * 2, 2)], place, r2_s.at[zd], r2_r.at[z], on_z(zd)).start()
        return 0

    lax.fori_loop(1, RING, spread, 0)
    out[:, pl.ds(64 * z, 64), :] = gz[pl.ds(2 * zh, 2)]

    def take_last(k, _):
        zz = (z + k) % RING
        landed(out.at[:, pl.ds(64 * zz, 64)], r2_r.at[zz])
        return 0

    lax.fori_loop(1, RING, take_last, 0)

    for j in range(3):
        for t in range(3):
            row, q = weight_piece(j, t)
            wait = functools.partial(sent, wt.at[pl.ds(row * GROUP, GROUP)], wz_s.at[j, t])
            if t < 2:
                wait()
            else:
                pl.when(row < 36)(wait)
    lat_out.wait_send()
    sent(lats.at[0], lat_s.at[2])
    for k in range(6):
        sent(wo.at[wo_rows], wo_s.at[k])
    for k in range(1, 4):
        sent(wbuf.at[0:4, y, x], wp_s.at[0, k])
        sent(wbuf.at[4:7, y, x], wp_s.at[1, k])
        sent(wbuf.at[0:4, y], wp_s.at[2, k])
        sent(wbuf.at[4:7, :, x], wp_s.at[3, k])

    def done_z(k, _):
        zz = (z + k) % RING
        for f in range(2):
            sent(att.at[f, pl.ds(64 * zz, 64)], za_s.at[f, zz])
        sent(gz.at[0:2], r2_s.at[zz])
        return 0

    lax.fori_loop(1, RING, done_z, 0)

    def done_plane(k, _):
        ii = (i + k) % PLANE
        sent(xs.at[ii], xy_s.at[ii])
        sent(gs.at[ii], r1_s.at[ii])
        return 0

    lax.fori_loop(1, PLANE, done_plane, 0)

    def done_sibling(k, _):
        sent(xt.at[0, k], sb_s.at[k])
        return 0

    lax.fori_loop(0, PLANE, done_sibling, 0)


def shards(
    latent,
    modulation,
    w_qkv_space,
    w_out_space,
    w_qkv_time,
    w_out_time,
    clip_frames,
    spatial_window,
):
    c = lax.axis_index("cfg")
    lat = latent.reshape(2, POSITIONS, WIDTH)
    wsp = jnp.transpose(w_qkv_space, (1, 0, 2))
    half = lax.dynamic_slice_in_dim(w_qkv_time, c * PAIR, PAIR, 2)
    wt = jnp.concatenate(
        [
            jnp.transpose(half, (1, 2, 0)).reshape(3 * PAIR, WIDTH),
            lax.dynamic_slice_in_dim(w_out_time, c * PAIR, PAIR, 0),
        ],
        axis=0,
    )
    dma = pltpu.SemaphoreType.DMA
    vmem = pl.BlockSpec(memory_space=pltpu.VMEM)
    smem = pl.BlockSpec(memory_space=pltpu.SMEM)
    out = pl.pallas_call(
        kernel,
        out_shape=jax.ShapeDtypeStruct((2, POSITIONS, HALF), BF),
        in_specs=[smem, smem] + [vmem] * 5,
        out_specs=vmem,
        scratch_shapes=[
            pltpu.VMEM((6, WIDTH), F32),
            pltpu.VMEM((8, 128), BF),
            pltpu.VMEM((POSITIONS, 384), BF),
            pltpu.VMEM((PAD + POSITIONS + PAD, 384), BF),
            pltpu.VMEM((PAD + POSITIONS + PAD, 384), BF),
            pltpu.VMEM((128, 384), F32),
            pltpu.VMEM((2, POSITIONS, 384), BF),
            pltpu.VMEM((4, 4, 64, 384), BF),
            pltpu.VMEM((4, LOCAL, WIDTH), BF),
            pltpu.VMEM((4, 64, WIDTH), BF),
            pltpu.VMEM((PLANE, 16, WIDTH), BF),
            pltpu.VMEM((2, PLANE, 16, WIDTH), BF),
            pltpu.VMEM((7, 4, 4, GROUP, WIDTH), BF),
            pltpu.VMEM((256, 256), F32),
            pltpu.VMEM((512, WIDTH), BF),
            pltpu.VMEM((4, 512, PAIR), BF),
            pltpu.VMEM((512, 640), BF),
            pltpu.VMEM((512, 640), BF),
            pltpu.VMEM((PLANE, 16, HALF), BF),
            pltpu.VMEM((PLANE, 16, HALF), BF),
            pltpu.VMEM((4, 64, HALF), BF),
            dma((2,)),
            dma((4,)),
            dma((6,)),
            dma((6,)),
            dma((3, 3)),
            dma((3, 3)),
            dma((4, 4)),
            dma((4, 4)),
            dma((2, RING)),
            dma((2, RING)),
            dma((PLANE,)),
            dma((PLANE,)),
            dma((PLANE,)),
            dma((PLANE,)),
            dma((2,)),
            dma((PLANE,)),
            dma((PLANE,)),
            dma((RING,)),
            dma((RING,)),
        ],
        compiler_params=pltpu.CompilerParams(
            collective_id=0, has_side_effects=True, vmem_limit_bytes=56 * 1024 * 1024
        ),
        name="sublayers",
    )(spatial_window, clip_frames, lat, modulation[0], wsp, w_out_space, wt)
    return out.reshape(2 * POSITIONS, HALF)


def solution(mesh):
    return jax.shard_map(
        shards,
        mesh=mesh,
        in_specs=(
            P("seq", None),
            P("cfg", None, None),
            P(None, None, "head"),
            P("head", None),
            P(None, None, "head"),
            P("head", None),
            P(),
            P(),
        ),
        out_specs=P("seq", "cfg"),
        check_vma=False,
    )
```

time: 492 us -> 132 us (0.27)
  blocking collectives: 234 us -> 0 us
  waiting for transfers between devices: 162 us -> 0 us
  Pallas kernels: 0 us -> 121 us
  matrix products: 27.5 us -> 0 us
  local copies, waits for them, and re-layouts: 26.3 us -> 9.16 us
  other arithmetic: 15.7 us -> 1.18 us
  between operations: 13.7 us -> 0.03 us
  starting transfers between devices: 11 us -> 0 us
    psum x1 -> x0, blocking collectives: 166 us -> none  [shards(): projected = lax.psum(partial_value, 'head').astype(jnp.bfloat16)]
    pallas_call x0 -> x1, Pallas kernels: none -> 121 us  [shards(): pl.pallas_call(kernel, out_shape=jax.ShapeDtypeStruct((2, POSITIONS, HALF...]
    psum x1 -> x0, waiting for transfers between devices: 119 us -> none  [shards(): summed = lax.psum(partial_time.astype(jnp.bfloat16), 'head')]
    all_to_all x1 -> x0, blocking collectives: 68.2 us -> none  [shards(): lax.all_to_all(result.reshape(groups, frame_dev, slab_rows, moved_width),...]
    all_to_all x1 -> x0, waiting for transfers between devices: 37.8 us -> none  [shards(): lax.all_to_all(columns, 'seq', split_axis=1, concat_axis=0, tiled=True)]
    dot_general x6 -> x0, matrix products: 18.5 us -> none  [the longest x1 4.24 us: shards(): jnp.einsum('fhqk,fkhd->fqhd', weights, packed[:, :, 2], preferred_element...]
    all_to_all x1 -> x0, starting transfers between devices: 11 us -> none  [shards(): lax.all_to_all(columns, 'seq', split_axis=1, concat_axis=0, tiled=True)]
    convert_element_type x5 -> x0, other arithmetic: 9.38 us -> none  [the longest x1 3.47 us: shards(): (uncond_vals + GUIDE * (cond_half.astype(jnp.float32) - uncond_vals)).ast...]
  transfers between devices with their start and end apart: 3 -> 0, of which waited for: 3 -> 0; matrix products, arithmetic and copies ran while one was open for 0% -> 0% of each run, Pallas kernels for 0% -> 0%
where the time goes in v1:
time: 132 us
  Pallas kernels  121 us (92%)
  local copies, waits for them, and re-layouts  9.16 us (7%)
    pallas_call x1, Pallas kernels, shards(): pl.pallas_call(kernel, out_shape=jax.ShapeDtypeStruct((2, POSITIONS, HALF...  121 us
    unnamed x4, local copies, waits for them, and re-layouts  5.7 us

profile of v1, /device:TPU:6, one launch (start us, length us, event | category | flops | bytes accessed | tf_op | source)
XLA Modules:
  0.0 131.5 jit_solution(17603654033561810423)
XLA Ops:
  0.0 0.0 copy-start
  0.0 1.5 %copy.13 = f32[1,6,1152]{2,1,0:T(8,128)} copy(f32[1,6,1152]{2,0,1:T(1,128)} %param.9) | data formatting | bytes 55296
  1.5 1.0 constant_dynamic-slice_fusion
  2.5 0.0 copy-done
  2.5 0.1 constant_dynamic-slice_fusion.1
  2.6 1.2 pad_maximum_fusion.wt
  3.8 4.2 %copy.9 = bf16[1152,3,288]{2,0,1:T(8,128)(2,1)} copy(bf16[1152,3,288]{0,2,1:T(8,128)(2,1)} %param.10) | data formatting | bytes 3981312 | tf_op args[2]
  8.0 121.1 %sublayers.1 = bf16[2,512,576]{2,1,0:T(8,128)(2,1)} custom-call(s32[512]{0:T(512)} %sw_ref.1, s32[4]{0:T(128)} %clip_ref.1, bf16[2,512,1152]{2,1,0:T(8,128)(2,1)} %bitcast.12, f32[6,1152]{1,0:T(8,128)} %bitcast.13, bf16[3,1152,288]{2,1,0:T(8,128)(2,1)} %bitcast.9, bf16[288,1152]{1,0:T(8,128)(2,1)} %wo.1, bf16[576,1152]{1,0:T(8,128)(2,1)} %pad_maximum_fusion.wt), custom_call_target="tpu_custom_call" | custom-call | tf_op jit(solution)/shard_map/sublayers/pallas_call | solution.py:463
  129.1 2.4 %copy.10 = bf16[1024,576]{0,1:T(8,128)(2,1)} copy(bf16[1024,576]{1,0:T(8,128)(2,1)} %bitcast.10) | data formatting | bytes 2359296 | tf_op jit(solution)/shard_map/reshape | solution.py:515
Async XLA Ops:
  0.0 2.5 %copy-start = (bf16[1152,3,288]{0,2,1:T(8,128)(2,1)S(1)}, bf16[1152,3,288]{0,2,1:T(8,128)(2,1)}, u32[]{:S(2)}) copy-start(bf16[1152,3,288]{0,2,1:T(8,128)(2,1)} %param.12) | copy-start | bytes 5971972

commit v2 on v1

--- a/solution.py
+++ b/solution.py
@@ -72,8 +72,8 @@
 
 def kernel(
     sw_ref, clip_ref, lat, mod, wsp, wo, wt, out,
-    modx, xb, qs, ks, vs, base, att, heads, wos, lats, xs, xt, wbuf, tbias, xn, os_, psend, precv, gs, g2, gz,
-    mod_s, lat_s, wo_s, wo_r, wz_s, wz_r, wp_s, wp_r, za_s, za_r, xy_s, xy_r, sb_s, sb_r, pp_s, r1_s, r1_r, r2_s, r2_r,
+    modx, qs, ks, vs, base, att, packed, heads, wsib, wos, lats, xs, xt, wbuf, tbias, xn, os_, psend, precv, gs, g2, gz, tr,
+    mod_s, lat_s, wz_s, wz_r, wp_s, wp_r, za_s, za_r, xy_s, xy_r, sb_s, sb_r, pp_s, r1_s, r1_r, r2_s, r2_r,
 ):
     c = lax.axis_index("cfg")
     s = lax.axis_index("seq")
@@ -119,26 +119,63 @@
     pl.semaphore_wait(barrier, RING - 1 + PLANE - 1 + 1)
 
     far = jnp.where(c == 0, 2, RING - 2)
-
-    def shard_rows(j):
-        return (i + 12 * j) % GROUP
-
-    def weight_piece(j, t):
-        first = shard_rows(j)
-        flat = 36 * j + first + 16 * t
-        return first + 16 * t, flat // 16
-
     hops = [RING - 1, far, 1]
-    for j in range(3):
-        for t in range(3):
-            row, q = weight_piece(j, t)
-            copy = remote(
-                wt.at[pl.ds(row * GROUP, GROUP)], wbuf.at[q, y, x], wz_s.at[j, t], wz_r.at[j, t], on_z((z + hops[j]) % RING)
-            )
-            if t < 2:
-                copy.start()
-            else:
-                pl.when(row < 36)(copy.start)
+
+    def piece_of(j, t):
+        if t == 0:
+            row = (i + 7 * j) % GROUP
+            return row, (9 * j + row) // 16, row < 9
+        row = (i + 12 * j) % GROUP + 16 * (t - 1)
+        return 9 + row, 2 + (36 * j + row) // 16, row < 36
+
+    def each_piece(step, act):
+        for j in range(3):
+            for t in step:
+                row, q, there = piece_of(j, t)
+                pl.when(there)(functools.partial(act, j, t, row, q))
+
+    def start_piece(j, t, row, q):
+        remote(
+            wt.at[pl.ds(row * GROUP, GROUP)], wbuf.at[q, y, x], wz_s.at[j, t], wz_r.at[j, t], on_z((z + hops[j]) % RING)
+        ).start()
+
+    def take_piece(j, t, row, q):
+        landed(wbuf.at[q, y, x], wz_r.at[j, t])
+
+    def sent_piece(j, t, row, q):
+        sent(wt.at[pl.ds(row * GROUP, GROUP)], wz_s.at[j, t])
+
+    each_piece([0], start_piece)
+    each_piece([1, 2, 3], start_piece)
+
+    pushed = []
+
+    def push(index, ref, dev):
+        remote(ref, ref, wp_s.at[index], wp_r.at[index], dev).start()
+        pushed.append((ref, index))
+
+    def first_phase(index, cut_a, cut_b):
+        for k in range(1, 4):
+            push(index + k - 1, wbuf.at[cut_a, y, x], on_plane(4 * y + (x + k) % 4))
+            push(index + k + 2, wbuf.at[cut_b, y, x], on_plane(4 * ((y + k) % 4) + x))
+
+    def first_landed(index, cut_a, cut_b):
+        for k in range(1, 4):
+            landed(wbuf.at[cut_a, y, (x + 4 - k) % 4], wp_r.at[index + k - 1])
+            landed(wbuf.at[cut_b, (y + 4 - k) % 4, x], wp_r.at[index + k + 2])
+
+    def second_phase(index, cut_a, cut_b, ks_):
+        for k in ks_:
+            push(index + k - 1, wbuf.at[cut_a, y], on_plane(4 * ((y + k) % 4) + x))
+            push(index + k + 2, wbuf.at[cut_b, :, x], on_plane(4 * y + (x + k) % 4))
+
+    def second_landed(index, cut_a, cut_b, ks_):
+        for k in ks_:
+            landed(wbuf.at[cut_a, (y + 4 - k) % 4], wp_r.at[index + k - 1])
+            landed(wbuf.at[cut_b, :, (x + 4 - k) % 4], wp_r.at[index + k + 2])
+
+    space_a, space_b = slice(0, 1), slice(1, 2)
+    time_a, time_b = slice(2, 6), slice(6, 9)
 
     mod_copy = remote(mod, modx, mod_s.at[0], mod_s.at[1], sib)
     mod_copy.start()
@@ -146,10 +183,6 @@
         lat.at[c, pl.ds(64 * (7 - z), 64)], lats.at[zh * 2 + c], lat_s.at[0], lat_s.at[1], on_z(7 - z)
     )
     lat_out.start()
-    wo_rows = pl.ds(PAIR * c, PAIR)
-    for k, hop in enumerate([1, RING - 1, far]):
-        remote(wo.at[wo_rows], wos.at[h, wo_rows], wo_s.at[k], wo_r.at[k], on_z((z + hop) % RING)).start()
-
     oy = jnp.int32(7)
     ox = jnp.int32(7)
     for r in range(1, 8):
@@ -181,12 +214,15 @@
         def project(rb, _):
             rows = pl.ds(rb * 256, 256)
             values = modulated(lat[f, rows, :], shift1, scale1)
-            qs[rows, 0:LOCAL] = dot(values, wsp[0]).astype(BF)
-            ks[pl.ds(PAD + rb * 256, 256), 0:LOCAL] = dot(values, wsp[1]).astype(BF)
-            vs[pl.ds(PAD + rb * 256, 256), 0:LOCAL] = dot(values, wsp[2]).astype(BF)
+            qs[rows, 0:LOCAL] = dot_t(values, wsp[0]).astype(BF)
+            ks[pl.ds(PAD + rb * 256, 256), 0:LOCAL] = dot_t(values, wsp[1]).astype(BF)
+            vs[pl.ds(PAD + rb * 256, 256), 0:LOCAL] = dot_t(values, wsp[2]).astype(BF)
             return 0
 
         lax.fori_loop(0, 2, project, 0)
+        if f == 0:
+            each_piece([0], take_piece)
+            first_phase(0, space_a, space_b)
 
         def attend(k, _):
             query = qs[pl.ds(k * 128, 128), :]
@@ -200,71 +236,66 @@
             total = mixed[0:128] * masks[0]
             for n in range(1, 4):
                 total = total + mixed[128 * n : 128 * (n + 1)] * masks[n]
-            att[f, pl.ds(k * 128, 128), :] = total.astype(BF)
             for t in range(2):
                 zd = 2 * k + t
-                block = att.at[f, pl.ds(64 * zd, 64)]
-                copy = remote(block, heads.at[h, zh * 2 + f], za_s.at[f, zd], za_r.at[f, z], on_z(zd))
+                part = total[64 * t : 64 * (t + 1)]
+                rest = part[0:16, 256:384]
+                for r in range(1, 4):
+                    rest = rest + pltpu.roll(part[16 * r : 16 * (r + 1), 256:384], 32 * r, 1)
+                whole = jnp.concatenate([part[:, 0:128], part[:, 128:256], rest], axis=0)
+                att[f, zd] = whole.astype(BF)
+                copy = remote(att.at[f, zd], packed.at[h, zh * 2 + f], za_s.at[f, zd], za_r.at[f, z], on_z(zd))
                 pl.when(zd != z)(copy.start)
 
                 @pl.when(zd == z)
                 def _():
-                    heads[h, zh * 2 + f] = att[f, pl.ds(64 * zd, 64), :]
+                    packed[h, zh * 2 + f] = att[f, zd]
 
             return 0
 
         lax.fori_loop(0, 4, attend, 0)
 
         if f == 0:
-            for j in range(3):
-                for t in range(3):
-                    row, q = weight_piece(j, t)
-                    wait = functools.partial(landed, wbuf.at[q, y, x], wz_r.at[j, t])
-                    if t < 2:
-                        wait()
-                    else:
-                        pl.when(row < 36)(wait)
-            for k in range(1, 4):
-                to_x = (x + k) % 4
-                to_y = (y + k) % 4
-                piece = wbuf.at[0:4, y, x]
-                remote(piece, piece, wp_s.at[0, k], wp_r.at[0, k], on_plane(4 * y + to_x)).start()
-                piece = wbuf.at[4:7, y, x]
-                remote(piece, piece, wp_s.at[1, k], wp_r.at[1, k], on_plane(4 * to_y + x)).start()
+            each_piece([1, 2, 3], take_piece)
+            first_phase(6, time_a, time_b)
+            first_landed(0, space_a, space_b)
+            second_phase(12, space_a, space_b, (1, 2, 3))
             piece = lats.at[(1 - zh) * 2 + c]
             landed(piece, lat_s.at[1])
             remote(piece, piece, lat_s.at[2], lat_s.at[3], sib).start()
 
-    for k in range(1, 4):
-        from_x = (x + 4 - k) % 4
-        from_y = (y + 4 - k) % 4
-        landed(wbuf.at[0:4, y, from_x], wp_r.at[0, k])
-        landed(wbuf.at[4:7, from_y, x], wp_r.at[1, k])
-    for k in range(1, 4):
-        to_x = (x + k) % 4
-        to_y = (y + k) % 4
-        piece = wbuf.at[0:4, y]
-        remote(piece, piece, wp_s.at[2, k], wp_r.at[2, k], on_plane(4 * to_y + x)).start()
-        piece = wbuf.at[4:7, :, x]
-        remote(piece, piece, wp_s.at[3, k], wp_r.at[3, k], on_plane(4 * y + to_x)).start()
-
-    for k, hop in enumerate([RING - 1, 1, 2]):
-        piece = wos.at[(h + hop) % 4, wo_rows]
-        landed(piece, wo_r.at[k])
-        remote(piece, piece, wo_s.at[3 + k], wo_r.at[3 + k], sib).start()
+    first_landed(6, time_a, time_b)
+    second_phase(18, time_a, time_b, (1, 3))
+    second_landed(12, space_a, space_b, (1, 2, 3))
+    remote(wbuf.at[0:2], wsib, wp_s.at[32], wp_r.at[32], sib).start()
     wos[h] = wo[...]
     lats[pl.ds(zh * 2, 2)] = lat[:, pl.ds(64 * z, 64), :]
     landed(lats.at[(1 - zh) * 2 + (1 - c)], lat_s.at[3])
-    for k, hop in enumerate([RING - 1, 1, 2]):
-        landed(wos.at[(h + hop) % 4, pl.ds(PAIR * (1 - c), PAIR)], wo_r.at[3 + k])
+    landed(wsib, wp_r.at[32])
+    for p in range(27):
+        shard, row = (h + 1 + p // 9) % 4, 16 * (p % 9)
+        place = (p // 16, (p % 16) // 4, p % 4)
+        wos[shard, pl.ds(PAIR * c + row, 16), :] = wbuf[place]
+        wos[shard, pl.ds(PAIR * (1 - c) + row, 16), :] = wsib[place]
 
     def take_heads(k, _):
         zz = (z + k) % RING
         for f in range(2):
-            landed(heads.at[zz % 4, (zz // 4) * 2 + f], za_r.at[f, zz])
+            landed(packed.at[zz % 4, (zz // 4) * 2 + f], za_r.at[f, zz])
         return 0
 
     lax.fori_loop(1, RING, take_heads, 0)
+
+    def unpack(k, _):
+        block = packed[k // 4, k % 4]
+        heads[k // 4, k % 4, :, 0:128] = block[0:64]
+        heads[k // 4, k % 4, :, 128:256] = block[64:128]
+        rest = block[128:144].astype(F32)
+        parts = [rest] + [pltpu.roll(rest, 128 - 32 * r, 1) for r in range(1, 4)]
+        heads[k // 4, k % 4, :, 256:384] = jnp.concatenate(parts, axis=0).astype(BF)
+        return 0
+
+    lax.fori_loop(0, 16, unpack, 0)
 
     gate1 = mod[2:3, :]
     order = jnp.where(iota((256, 256), 1) == (iota((256, 256), 0) % 4) * 64 + iota((256, 256), 0) // 4, 1.0, 0.0).astype(BF)
@@ -282,6 +313,11 @@
         return 0
 
     lax.fori_loop(1, PLANE, give, 0)
+    second_landed(18, time_a, time_b, (1, 3))
+    push(24, wbuf.at[2:4, (y + 3) % 4], on_plane(4 * ((y + 1) % 4) + x))
+    push(25, wbuf.at[4:6, (y + 1) % 4], on_plane(4 * ((y + 3) % 4) + x))
+    push(26, wbuf.at[6:7, :, (x + 3) % 4], on_plane(4 * y + (x + 1) % 4))
+    push(27, wbuf.at[7:9, :, (x + 1) % 4], on_plane(4 * y + (x + 3) % 4))
     xt[0, i] = xs[i]
     remote(xs.at[i], xt.at[1, i], sb_s.at[i], sb_r.at[i], sib).start()
 
@@ -303,17 +339,19 @@
     mod_copy.wait()
     xn[256:512, :] = modulated(xt[1].reshape(256, WIDTH), modx[3:4, :], modx[4:5, :])
 
-    for k in range(1, 4):
-        from_x = (x + 4 - k) % 4
-        from_y = (y + 4 - k) % 4
-        landed(wbuf.at[0:4, from_y], wp_r.at[2, k])
-        landed(wbuf.at[4:7, :, from_x], wp_r.at[3, k])
+    landed(wbuf.at[2:4, (y + 2) % 4], wp_r.at[24])
+    landed(wbuf.at[4:6, (y + 2) % 4], wp_r.at[25])
+    landed(wbuf.at[6:7, :, (x + 2) % 4], wp_r.at[26])
+    landed(wbuf.at[7:9, :, (x + 2) % 4], wp_r.at[27])
+
+    def at_flat(flat):
+        return 2 + flat // 16, (flat % 16) // 4, flat % 4
 
     def weight_rows(slot, first, count):
         if slot == 0:
-            return wt[first * 16 : (first + count) * 16, :]
+            return wt[(9 + first) * 16 : (9 + first + count) * 16, :]
         flat = 36 * (slot - 1) + first
-        return jnp.concatenate([wbuf[p // 16, (p % 16) // 4, p % 4] for p in range(flat, flat + count)], axis=0)
+        return jnp.concatenate([wbuf[at_flat(p)] for p in range(flat, flat + count)], axis=0)
 
     pair_masks = [head_mask(n, PAIR) for n in range(2)]
     for slot in range(4):
@@ -332,11 +370,11 @@
         total = jnp.zeros((512, 640), F32)
         for slot in range(4):
             if slot == 0:
-                weights = wt[27 * 16 : 36 * 16, pl.ds(first, 640)]
+                weights = wt[36 * 16 : 45 * 16, pl.ds(first, 640)]
             else:
                 flat = 36 * (slot - 1) + 27
                 weights = jnp.concatenate(
-                    [wbuf[p // 16, (p % 16) // 4, p % 4, :, pl.ds(first, 640)] for p in range(flat, flat + 9)], axis=0
+                    [wbuf[at_flat(p) + (slice(None), pl.ds(first, 640))] for p in range(flat, flat + 9)], axis=0
                 )
             total = total + dot(os_[slot], weights)
         return total
@@ -378,45 +416,69 @@
     order = jnp.where(iota((256, 256), 1) == (iota((256, 256), 0) % 64) * 4 + iota((256, 256), 0) // 64, 1.0, 0.0).astype(BF)
     gz[...] = dot(order, g2[...].reshape(256, HALF)).astype(BF).reshape(4, 64, HALF)
 
-    def spread(k, _):
-        zd = (z + k) % RING
-        place = out.at[:, pl.ds(64 * z, 64)]
-        remote(gz.at[pl.ds((zd // 4) * 2, 2)], place, r2_s.at[zd], r2_r.at[z], on_z(zd)).start()
-        return 0
-
-    lax.fori_loop(1, RING, spread, 0)
+    left, right = on_z((z + RING - 1) % RING), on_z((z + 1) % RING)
+    own_block, other_block = gz.at[pl.ds(2 * zh, 2)], gz.at[pl.ds(2 * (1 - zh), 2)]
+
+    def slot(zz):
+        return out.at[:, pl.ds(64 * zz, 64)]
+
+    def inner(hh):
+        return zh * 4 + hh
+
+    def outer(hh):
+        return (1 - zh) * 4 + hh
+
     out[:, pl.ds(64 * z, 64), :] = gz[pl.ds(2 * zh, 2)]
-
-    def take_last(k, _):
-        zz = (z + k) % RING
-        landed(out.at[:, pl.ds(64 * zz, 64)], r2_r.at[zz])
-        return 0
-
-    lax.fori_loop(1, RING, take_last, 0)
-
-    for j in range(3):
-        for t in range(3):
-            row, q = weight_piece(j, t)
-            wait = functools.partial(sent, wt.at[pl.ds(row * GROUP, GROUP)], wz_s.at[j, t])
-            if t < 2:
-                wait()
+    for role in range(4):
+
+        @pl.when(h == role)
+        def _():
+            waits = []
+
+            def go(side, src, zz, index, transit=False):
+                dst = tr if transit else slot(zz)
+                recv = r2_r.at[RING] if transit else r2_r.at[zz]
+                remote(src, dst, r2_s.at[side, index], recv, [left, right][side]).start()
+                waits.append((side, index))
+
+            def event(side, zz, forward):
+                landed(slot(zz), r2_r.at[zz])
+                if forward:
+                    go(side, slot(zz), zz, zz)
+
+            if role < 2:
+                go(0, other_block, z, RING, transit=role == 1)
             else:
-                pl.when(row < 36)(wait)
+                go(1, other_block, z, RING, transit=role == 2)
+            if role > 0:
+                go(0, own_block, z, z)
+            if role < 3:
+                go(1, own_block, z, z)
+            if role in (0, 3):
+                landed(tr, r2_r.at[RING])
+                source = inner(1 if role == 0 else 2)
+                go(0 if role == 0 else 1, tr, source, source)
+            lefts = [inner(k) for k in range(role + 1, 4)] + [outer(0), outer(1)]
+            rights = [inner(k) for k in range(role - 1, -1, -1)] + [outer(3), outer(2)]
+            for k in range(max(len(lefts), len(rights))):
+                if k < len(lefts):
+                    event(0, lefts[k], role > 0)
+                if k < len(rights):
+                    event(1, rights[k], role < 3)
+            for side, index in waits:
+                sent(gz.at[0:2], r2_s.at[side, index])
+
+    each_piece([0, 1, 2, 3], sent_piece)
     lat_out.wait_send()
     sent(lats.at[0], lat_s.at[2])
-    for k in range(6):
-        sent(wo.at[wo_rows], wo_s.at[k])
-    for k in range(1, 4):
-        sent(wbuf.at[0:4, y, x], wp_s.at[0, k])
-        sent(wbuf.at[4:7, y, x], wp_s.at[1, k])
-        sent(wbuf.at[0:4, y], wp_s.at[2, k])
-        sent(wbuf.at[4:7, :, x], wp_s.at[3, k])
+    for ref, index in pushed:
+        sent(ref, wp_s.at[index])
+    sent(wsib, wp_s.at[32])
 
     def done_z(k, _):
         zz = (z + k) % RING
         for f in range(2):
-            sent(att.at[f, pl.ds(64 * zz, 64)], za_s.at[f, zz])
-        sent(gz.at[0:2], r2_s.at[zz])
+            sent(att.at[f, zz], za_s.at[f, zz])
         return 0
 
     lax.fori_loop(1, RING, done_z, 0)
@@ -448,10 +510,11 @@
 ):
     c = lax.axis_index("cfg")
     lat = latent.reshape(2, POSITIONS, WIDTH)
-    wsp = jnp.transpose(w_qkv_space, (1, 0, 2))
+    wsp = jnp.transpose(w_qkv_space, (1, 2, 0))
     half = lax.dynamic_slice_in_dim(w_qkv_time, c * PAIR, PAIR, 2)
     wt = jnp.concatenate(
         [
+            lax.dynamic_slice_in_dim(w_out_space, c * PAIR, PAIR, 0),
             jnp.transpose(half, (1, 2, 0)).reshape(3 * PAIR, WIDTH),
             lax.dynamic_slice_in_dim(w_out_time, c * PAIR, PAIR, 0),
         ],
@@ -467,18 +530,19 @@
         out_specs=vmem,
         scratch_shapes=[
             pltpu.VMEM((6, WIDTH), F32),
-            pltpu.VMEM((8, 128), BF),
             pltpu.VMEM((POSITIONS, 384), BF),
             pltpu.VMEM((PAD + POSITIONS + PAD, 384), BF),
             pltpu.VMEM((PAD + POSITIONS + PAD, 384), BF),
             pltpu.VMEM((128, 384), F32),
-            pltpu.VMEM((2, POSITIONS, 384), BF),
+            pltpu.VMEM((2, RING, 144, 128), BF),
+            pltpu.VMEM((4, 4, 144, 128), BF),
             pltpu.VMEM((4, 4, 64, 384), BF),
+            pltpu.VMEM((2, 4, 4, GROUP, WIDTH), BF),
             pltpu.VMEM((4, LOCAL, WIDTH), BF),
             pltpu.VMEM((4, 64, WIDTH), BF),
             pltpu.VMEM((PLANE, 16, WIDTH), BF),
             pltpu.VMEM((2, PLANE, 16, WIDTH), BF),
-            pltpu.VMEM((7, 4, 4, GROUP, WIDTH), BF),
+            pltpu.VMEM((9, 4, 4, GROUP, WIDTH), BF),
             pltpu.VMEM((256, 256), F32),
             pltpu.VMEM((512, WIDTH), BF),
             pltpu.VMEM((4, 512, PAIR), BF),
@@ -487,14 +551,13 @@
             pltpu.VMEM((PLANE, 16, HALF), BF),
             pltpu.VMEM((PLANE, 16, HALF), BF),
             pltpu.VMEM((4, 64, HALF), BF),
+            pltpu.VMEM((2, 64, HALF), BF),
             dma((2,)),
             dma((4,)),
-            dma((6,)),
-            dma((6,)),
-            dma((3, 3)),
-            dma((3, 3)),
-            dma((4, 4)),
-            dma((4, 4)),
+            dma((3, 4)),
+            dma((3, 4)),
+            dma((33,)),
+            dma((33,)),
             dma((2, RING)),
             dma((2, RING)),
             dma((PLANE,)),
@@ -504,8 +567,8 @@
             dma((2,)),
             dma((PLANE,)),
             dma((PLANE,)),
-            dma((RING,)),
-            dma((RING,)),
+            dma((2, RING + 1)),
+            dma((RING + 1,)),
         ],
         compiler_params=pltpu.CompilerParams(
             collective_id=0, has_side_effects=True, vmem_limit_bytes=56 * 1024 * 1024

time: 132 us -> 121 us (0.917)
  Pallas kernels: 121 us -> 114 us
  local copies, waits for them, and re-layouts: 9.16 us -> 4.83 us
    pallas_call x1, Pallas kernels: 121 us -> 114 us  [shards(): pl.pallas_call(kernel, out_shape=jax.ShapeDtypeStruct((2, POSITIONS, HALF...]
    unnamed x4 -> x5, local copies, waits for them, and re-layouts: 5.7 us -> 1.11 us
where the time goes in v2:
time: 121 us; the launch traced here: 120 us
  Pallas kernels  114 us (94%)
  local copies, waits for them, and re-layouts  4.83 us (4%)
  other arithmetic  1.3 us (1%)
    pallas_call x1, Pallas kernels, shards(): pl.pallas_call(kernel, out_shape=jax.ShapeDtypeStruct((2, POSITIONS, HALF...  114 us

profile of v2, /device:TPU:6, one launch (start us, length us, event | category | flops | bytes accessed | tf_op | source)
XLA Modules:
  0.0 120.3 jit_solution(2778437664621856062)
XLA Ops:
  0.0 0.0 copy-start
  0.0 1.3 %constant_dynamic-slice_fusion = (bf16[144,1152]{1,0:T(8,128)(2,1)S(1)}, bf16[144,1152]{1,0:T(8,128)(2,1)S(1)}) fusion(bf16[288,1152]{1,0:T(8,128)(2,1)} %param.13, s32[]{:T(128)S(6)} %select_n.2, bf16[288,1152]{1,0:T(8,128)(2,1)} %wo.1), kind=kLoop, calls=%fused_computation.2 | loop fusion | bytes 1327108 | tf_op jit(solution)/shard_map/dynamic_slice | solution.py:519
  1.3 0.5 copy-done
  1.8 0.1 constant_dynamic-slice_fusion.1
  1.8 0.0 copy-start.1
  1.8 1.3 %pad_maximum_fusion.wt = bf16[720,1152]{1,0:T(8,128)(2,1)} fusion(bf16[144,1152]{1,0:T(8,128)(2,1)S(1)} %get-tuple-element.5, bf16[432,1152]{1,0:T(8,128)(2,1)S(1)} %bitcast.10, bf16[144,1152]{1,0:T(8,128)(2,1)S(1)} %get-tuple-element.6), kind=kLoop, calls=%fused_computation | loop fusion | flops 4976640 | bytes 3317760 | tf_op jit(solution)/shard_map/concatenate | solution.py:515
  3.1 0.0 copy-done.1
  3.2 0.6 copy.12
  3.8 114.1 %sublayers.1 = bf16[2,512,576]{2,1,0:T(8,128)(2,1)} custom-call(s32[512]{0:T(512)} %sw_ref.1, s32[4]{0:T(128)} %clip_ref.1, bf16[2,512,1152]{2,1,0:T(8,128)(2,1)} %bitcast.11, f32[6,1152]{1,0:T(8,128)} %bitcast.13, bf16[3,288,1152]{2,1,0:T(8,128)(2,1)} %bitcast.12, bf16[288,1152]{1,0:T(8,128)(2,1)} %wo.1, bf16[720,1152]{1,0:T(8,128)(2,1)} %pad_maximum_fusion.wt), custom_call_target="tpu_custom_call" | custom-call | tf_op jit(solution)/shard_map/sublayers/pallas_call | solution.py:526
  117.9 2.4 %copy.9 = bf16[1024,576]{0,1:T(8,128)(2,1)} copy(bf16[1024,576]{1,0:T(8,128)(2,1)} %bitcast.9) | data formatting | bytes 2359296 | tf_op jit(solution)/shard_map/reshape | solution.py:578
Async XLA Ops:
  0.0 1.8 %copy-start = (bf16[1152,3,288]{0,2,1:T(8,128)(2,1)S(1)}, bf16[1152,3,288]{0,2,1:T(8,128)(2,1)}, u32[]{:S(2)}) copy-start(bf16[1152,3,288]{0,2,1:T(8,128)(2,1)} %param.12) | copy-start | bytes 5971972
  1.8 1.3 %copy-start.1 = (f32[1,6,1152]{2,0,1:T(1,128)S(1)}, f32[1,6,1152]{2,0,1:T(1,128)}, u32[]{:S(2)}) copy-start(f32[1,6,1152]{2,0,1:T(1,128)} %param.9) | copy-start | bytes 82948

commit v3 on v2

v3 whole, which is shorter than its diff:
```python
import functools

import jax
import jax.numpy as jnp
from jax import lax
from jax.experimental import pallas as pl
from jax.experimental.pallas import tpu as pltpu
from jax.sharding import PartitionSpec as P

MESH = pl.DeviceIdType.MESH
HEAD_DIM = 72
POSITIONS = 512
WIDTH = 1152
HALF = 576
LOCAL = 288
PAIR = 144
TWIN = 16
GUIDE = 4.0
EPSILON = 1e-06
NEG = -1e30
PAD = 128
RING = 8
PLANE = 16
GROUP = 16
EXP_SCALE = HEAD_DIM ** (-0.5) * 1.4426950408889634
BF = jnp.bfloat16
F32 = jnp.float32


def iota(shape, dim):
    return lax.broadcasted_iota(jnp.int32, shape, dim)


def modulated(rows, shift, scale):
    values = rows.astype(F32)
    centred = values - jnp.mean(values, axis=-1, keepdims=True)
    spread = jnp.mean(centred * centred, axis=-1, keepdims=True)
    normed = centred * lax.rsqrt(spread + EPSILON)
    return (normed * (1.0 + scale) + shift).astype(BF)


def softmax_keys(scores):
    top = jnp.max(scores, axis=0, keepdims=True)
    terms = jnp.exp2((scores - top) * EXP_SCALE)
    return terms.astype(BF), 1.0 / jnp.sum(terms, axis=0, keepdims=True)


def dot(a, b):
    return lax.dot_general(a, b, (((1,), (0,)), ((), ())), preferred_element_type=F32)


def dot_t(a, b):
    return lax.dot_general(a, b, (((1,), (1,)), ((), ())), preferred_element_type=F32)


def dot_first(a, b):
    return lax.dot_general(a, b, (((0,), (0,)), ((), ())), preferred_element_type=F32)


def head_mask(head, first, rows):
    row = iota((rows, 1), 0) + first
    return jnp.where((row >= head * HEAD_DIM) & (row < (head + 1) * HEAD_DIM), 1.0, 0.0).astype(BF)


def frame_window(frame, clip_ref):
    ends = [clip_ref[0]]
    for j in range(1, 4):
        ends.append(ends[-1] + clip_ref[j])
    clip = jnp.zeros_like(frame)
    start = jnp.zeros_like(frame)
    for end in ends:
        clip = clip + jnp.where(frame >= end, 1, 0)
        start = jnp.where(frame >= end, end, start)
    return clip * 64 + (frame - start) // TWIN


def kernel(
    sw_ref, clip_ref, lat, mod, wsp, wo, wt, out,
    modx, qt, ks, vt, base, att, heads, wsib, wos, lats, xs, xt, wbuf, tbias, xn, ot, psend, precv, gs, g2, gz, tr,
    mod_s, lat_s, wz_s, wz_r, wp_s, wp_r, za_s, za_r, xy_s, xy_r, sb_s, sb_r, pp_s, r1_s, r1_r, r2_s, r2_r,
):
    c = lax.axis_index("cfg")
    s = lax.axis_index("seq")
    h = lax.axis_index("head")
    zh = s // PLANE
    i = s % PLANE
    y = i // 4
    x = i % 4
    z = zh * 4 + h

    def on_z(zz):
        return (c, (zz // 4) * PLANE + i, zz % 4)

    def on_plane(ii):
        return (c, zh * PLANE + ii, h)

    sib = (1 - c, s, h)
    left, right = on_z((z + RING - 1) % RING), on_z((z + 1) % RING)

    def remote(src, dst, send, recv, dev):
        return pltpu.make_async_remote_copy(
            src_ref=src, dst_ref=dst, send_sem=send, recv_sem=recv, device_id=dev, device_id_type=MESH
        )

    def landed(buf, recv):
        remote(buf, buf, recv, recv, sib).wait_recv()

    def sent(buf, send):
        remote(buf, buf, send, send, sib).wait_send()

    barrier = pltpu.get_barrier_semaphore()

    def greet_z(k, _):
        pl.semaphore_signal(barrier, inc=1, device_id=on_z((z + k) % RING), device_id_type=MESH)
        return 0

    def greet_plane(k, _):
        pl.semaphore_signal(barrier, inc=1, device_id=on_plane((i + k) % PLANE), device_id_type=MESH)
        return 0

    lax.fori_loop(1, RING, greet_z, 0)
    lax.fori_loop(1, PLANE, greet_plane, 0)
    pl.semaphore_signal(barrier, inc=1, device_id=sib, device_id_type=MESH)
    pl.semaphore_wait(barrier, RING - 1 + PLANE - 1 + 1)

    far = jnp.where(c == 0, 2, RING - 2)
    hops = [RING - 1, far, 1]
    index_a, index_b = 4 * y + x, 4 * x + y
    SPACE = [(0, index_a, 0, 9, [0, 1]), (1, index_b, 0, 9, [1, 2])]
    TIME = [
        (3, index_a, 2, 36, [0]),
        (4, index_a, 2, 36, [0, 1]),
        (5, index_a, 2, 36, [1]),
        (6, index_b, 2, 36, [1, 2]),
        (7, index_b, 2, 36, [2]),
    ]

    def each_sent(rows, act):
        for q, place, first, per, slots in rows:
            flat = 16 * (q - first) + place
            for j in slots:
                source = wt.at[(9 if per == 36 else 0) + flat - per * j]
                pl.when(flat // per == j)(functools.partial(act, q, place, j, source))

    def start_piece(q, place, j, source):
        remote(source, wbuf.at[q, place], wz_s.at[q, j], wz_r.at[q], on_z((z + hops[j]) % RING)).start()

    def sent_piece(q, place, j, source):
        sent(source, wz_s.at[q, j])

    def take_pieces(rows):
        for q, place, first, per, _ in rows:
            there = 16 * (q - first) + place < 3 * per
            pl.when(there)(functools.partial(landed, wbuf.at[q, place], wz_r.at[q]))

    each_sent(SPACE, start_piece)

    pushed = []

    def push(index, ref, dev):
        remote(ref, ref, wp_s.at[index], wp_r.at[index], dev).start()
        pushed.append((ref, index))

    def first_phase(index, cut_a, cut_b):
        for k in range(1, 4):
            push(index + k - 1, wbuf.at[cut_a, index_a], on_plane(4 * y + (x + k) % 4))
            push(index + k + 2, wbuf.at[cut_b, index_b], on_plane(4 * ((y + k) % 4) + x))

    def first_landed(index, cut_a, cut_b):
        for k in range(1, 4):
            landed(wbuf.at[cut_a, 4 * y + (x + 4 - k) % 4], wp_r.at[index + k - 1])
            landed(wbuf.at[cut_b, 4 * x + (y + 4 - k) % 4], wp_r.at[index + k + 2])

    def second_phase(index, cut_a, cut_b, steps):
        for k in steps:
            push(index + k - 1, wbuf.at[cut_a, pl.ds(4 * y, 4)], on_plane(4 * ((y + k) % 4) + x))
            push(index + k + 2, wbuf.at[cut_b, pl.ds(4 * x, 4)], on_plane(4 * y + (x + k) % 4))

    def second_landed(index, cut_a, cut_b, steps):
        for k in steps:
            landed(wbuf.at[cut_a, pl.ds(4 * ((y + 4 - k) % 4), 4)], wp_r.at[index + k - 1])
            landed(wbuf.at[cut_b, pl.ds(4 * ((x + 4 - k) % 4), 4)], wp_r.at[index + k + 2])

    space_a, space_b = slice(0, 1), slice(1, 2)
    time_a, time_b = slice(3, 6), slice(6, 8)

    mod_copy = remote(mod, modx, mod_s.at[0], mod_s.at[1], sib)
    mod_copy.start()
    lat_out = remote(
        lat.at[c, pl.ds(64 * (7 - z), 64)], lats.at[zh * 2 + c], lat_s.at[0], lat_s.at[1], on_z(7 - z)
    )
    oy = jnp.int32(7)
    ox = jnp.int32(7)
    for r in range(1, 8):
        oy = oy - jnp.where(sw_ref[16 * r] < 3, 1, 0)
        ox = ox - jnp.where(sw_ref[r] < 1, 1, 0)
    qj = iota((384, 128), 1)
    ki = iota((384, 128), 0)
    same = ((qj // 16 + 8 + oy) // 8 == (ki // 16 + oy) // 8) & ((qj % 16 + ox) // 8 == (ki % 16 + ox) // 8)
    base[...] = jnp.where(same, 0.0, NEG)

    def time_key(row):
        four = row % 4
        frame = (four // 2) * 32 + 2 * (row // 16) + four % 2
        return frame_window(frame, clip_ref) * 4 + (row % 16) // 4

    tbias[...] = jnp.where(time_key(iota((256, 1), 0)) == time_key(iota((1, 256), 1)), 0.0, NEG)

    for f in range(2):
        ks[f, 0:PAD, :] = jnp.zeros((PAD, 384), BF)
        ks[f, PAD + POSITIONS :, :] = jnp.zeros((PAD, 384), BF)
        ks[f, PAD : PAD + POSITIONS, 256:384] = jnp.zeros((POSITIONS, 128), BF)
        vt[f, :, 0:PAD] = jnp.zeros((LOCAL, PAD), BF)
        vt[f, :, PAD + POSITIONS :] = jnp.zeros((LOCAL, PAD), BF)
        qt[f, LOCAL:384, :] = jnp.zeros((384 - LOCAL, POSITIONS), BF)

    shift1, scale1 = mod[0:1, :], mod[1:2, :]
    masks = [head_mask(0, 0, 256), head_mask(1, 0, 256), head_mask(2, 0, 256), head_mask(3, 128, 256)]

    for f in range(2):
        for rb in range(2):
            rows = slice(rb * 256, (rb + 1) * 256)
            values = modulated(lat[f, rows, :], shift1, scale1)
            qt[f, 0:LOCAL, rows] = dot_t(wsp[0], values).astype(BF)
            ks[f, PAD + rb * 256 : PAD + (rb + 1) * 256, 0:LOCAL] = dot_t(values, wsp[1]).astype(BF)
            vt[f, :, PAD + rb * 256 : PAD + (rb + 1) * 256] = dot_t(wsp[2], values).astype(BF)
        if f == 0:
            take_pieces(SPACE)
            first_phase(0, space_a, space_b)
            each_sent(TIME, start_piece)
            lat_out.start()

    low = iota((1, 128), 1) < 64

    def attend(k, f):
        cols = pl.ds(pl.multiple_of(k * 128, 128), 128)
        around = pl.ds(pl.multiple_of(k * 128, 128), 384)
        keys = ks[f, around, :]
        query = qt[f, :, cols]
        three = jnp.concatenate([query[0:256] * m for m in masks[0:3]], axis=1)
        row = 8 * k - 8 + iota((384, 1), 0) // 16
        bias = base[...] + jnp.where((row >= 0) & (row < 32), 0.0, NEG)
        scores = jnp.concatenate(
            [dot(keys[:, 0:256], three), dot(keys[:, 128:384], query[128:384] * masks[3])], axis=1
        ) + jnp.concatenate([bias] * 4, axis=1)
        weights, over = softmax_keys(scores)
        mixed = dot(vt[f, :, around], weights)
        parts = [
            mixed[HEAD_DIM * n : HEAD_DIM * (n + 1), 128 * n : 128 * (n + 1)] * over[:, 128 * n : 128 * (n + 1)]
            for n in range(4)
        ]
        return jnp.concatenate(parts, axis=0)

    for step in range(2):
        for k in (2 * step, 2 * step + 1):
            first, second = attend(k, 0), attend(k, 1)
            att[2 * k] = jnp.where(low, first, pltpu.roll(second, 64, 1)).astype(BF)
            att[2 * k + 1] = jnp.where(low, pltpu.roll(first, 64, 1), second).astype(BF)
        for zd in range(4 * step, 4 * step + 4):
            place = heads.at[pl.ds(LOCAL * h, LOCAL), pl.ds(pl.multiple_of(128 * zh, 128), 128)]
            copy = remote(att.at[zd], place, za_s.at[zd], za_r.at[z], on_z(zd))
            pl.when(z != zd)(copy.start)

            @pl.when(z == zd)
            def _():
                heads[pl.ds(LOCAL * h, LOCAL), pl.ds(pl.multiple_of(128 * zh, 128), 128)] = att[zd]

        if step == 0:
            first_landed(0, space_a, space_b)
            second_phase(12, space_a, space_b, (1, 2, 3))
            take_pieces(TIME)
            first_phase(6, time_a, time_b)

    piece = lats.at[(1 - zh) * 2 + c]
    landed(piece, lat_s.at[1])
    remote(piece, piece, lat_s.at[2], lat_s.at[3], sib).start()
    first_landed(6, time_a, time_b)
    second_phase(18, time_a, time_b, (1, 3))
    second_landed(12, space_a, space_b, (1, 2, 3))
    remote(wbuf.at[0:2], wsib, wp_s.at[32], wp_r.at[32], sib).start()
    wos[h] = wo[...]
    lats[pl.ds(zh * 2, 2)] = lat[:, pl.ds(64 * z, 64), :]
    landed(lats.at[(1 - zh) * 2 + (1 - c)], lat_s.at[3])
    landed(wsib, wp_r.at[32])
    for p in range(27):
        shard, row = (h + 1 + p // 9) % 4, 16 * (p % 9)
        place = (p // 16, p % 16)
        wos[shard, pl.ds(PAIR * c + row, 16), :] = wbuf[place]
        wos[shard, pl.ds(PAIR * (1 - c) + row, 16), :] = wsib[place]

    def take_heads(k, _):
        zz = (z + k) % RING
        landed(heads.at[pl.ds(LOCAL * (zz % 4), LOCAL), pl.ds(pl.multiple_of(128 * (zz // 4), 128), 128)], za_r.at[zz])
        return 0

    lax.fori_loop(1, RING, take_heads, 0)

    straight = [
        remote(wt.at[9:25], wbuf.at[2], wp_s.at[28], wp_r.at[28], left),
        remote(wt.at[33:45], wbuf.at[8, 0:12], wp_s.at[29], wp_r.at[29], right),
    ]
    for copy in straight:
        copy.start()

    gate1 = mod[2:3, :]
    order = jnp.where(iota((256, 256), 1) == (iota((256, 256), 0) % 4) * 64 + iota((256, 256), 0) // 4, 1.0, 0.0).astype(BF)
    for n in range(3):
        cols = slice(384 * n, 384 * (n + 1))
        total = dot_first(heads[...], wos[:, :, cols].reshape(WIDTH, 384))
        after = lats[:, :, cols].reshape(256, 384).astype(F32) + gate1[:, cols] * total.astype(BF).astype(F32)
        xs[:, :, cols] = dot(order, after.astype(BF)).astype(BF).reshape(PLANE, 16, 384)

    def give(k, _):
        to = (i + k) % PLANE
        remote(xs.at[to], xt.at[0, i], xy_s.at[to], xy_r.at[i], on_plane(to)).start()
        return 0

    lax.fori_loop(1, PLANE, give, 0)
    second_landed(18, time_a, time_b, (1, 3))
    push(24, wbuf.at[time_a, pl.ds(4 * ((y + 3) % 4), 2)], on_plane(4 * ((y + 1) % 4) + x))
    push(25, wbuf.at[time_a, pl.ds(4 * ((y + 1) % 4) + 2, 2)], on_plane(4 * ((y + 3) % 4) + x))
    push(26, wbuf.at[time_b, pl.ds(4 * ((x + 3) % 4), 2)], on_plane(4 * y + (x + 1) % 4))
    push(27, wbuf.at[time_b, pl.ds(4 * ((x + 1) % 4) + 2, 2)], on_plane(4 * y + (x + 3) % 4))
    xt[0, i] = xs[i]
    remote(xs.at[i], xt.at[1, i], sb_s.at[i], sb_r.at[i], sib).start()

    def pass_on(k, _):
        source = (i + PLANE - k) % PLANE
        piece = xt.at[0, source]
        landed(piece, xy_r.at[source])
        remote(piece, xt.at[1, source], sb_s.at[source], sb_r.at[source], sib).start()
        return 0

    lax.fori_loop(1, PLANE, pass_on, 0)
    xn[0:256, :] = modulated(xt[0].reshape(256, WIDTH), mod[3:4, :], mod[4:5, :])

    def take_sibling(k, _):
        landed(xt.at[1, k], sb_r.at[k])
        return 0

    lax.fori_loop(0, PLANE, take_sibling, 0)
    mod_copy.wait()
    xn[256:512, :] = modulated(xt[1].reshape(256, WIDTH), modx[3:4, :], modx[4:5, :])

    landed(wbuf.at[time_a, pl.ds(4 * ((y + 2) % 4), 2)], wp_r.at[24])
    landed(wbuf.at[time_a, pl.ds(4 * ((y + 2) % 4) + 2, 2)], wp_r.at[25])
    landed(wbuf.at[time_b, pl.ds(4 * ((x + 2) % 4), 2)], wp_r.at[26])
    landed(wbuf.at[time_b, pl.ds(4 * ((x + 2) % 4) + 2, 2)], wp_r.at[27])
    for copy in straight:
        copy.wait()

    def groups(slot, first, count):
        if slot == 0:
            return [wt.at[9 + first + p] for p in range(count)]
        flats = range(36 * (slot - 1) + first, 36 * (slot - 1) + first + count)
        return [wbuf.at[2 + flat // 16, flat % 16] for flat in flats]

    pair_masks = [head_mask(n, 0, PAIR) for n in range(2)]
    for slot in range(4):
        weights = jnp.concatenate([ref[...] for ref in groups(slot, 0, 27)], axis=0)
        three = dot_t(weights, xn[...]).astype(BF)
        for b in range(2):
            cols = slice(256 * b, 256 * (b + 1))
            query, keys, vals = [three[PAIR * n : PAIR * (n + 1), cols] for n in range(3)]
            stacked = jnp.concatenate([query * m for m in pair_masks], axis=1)
            scores = dot_first(keys, stacked) + jnp.concatenate([tbias[...]] * 2, axis=1)
            terms, over = softmax_keys(scores)
            mixed = dot(vals, terms)
            parts = [
                mixed[HEAD_DIM * n : HEAD_DIM * (n + 1), 256 * n : 256 * (n + 1)] * over[:, 256 * n : 256 * (n + 1)]
                for n in range(2)
            ]
            ot[PAIR * slot : PAIR * (slot + 1), cols] = jnp.concatenate(parts, axis=0).astype(BF)

    def share(first):
        refs = [ref for slot in range(4) for ref in groups(slot, 27, 9)]
        return dot_first(ot[...], jnp.concatenate([ref[:, pl.ds(first, 640)] for ref in refs], axis=0))

    theirs = pl.multiple_of(512 * (1 - c), 128)
    mine = pl.multiple_of(512 * c, 128)
    psend[...] = share(theirs).astype(BF)
    give_share = remote(psend, precv, pp_s.at[0], pp_s.at[1], sib)
    give_share.start()
    own = share(mine)
    give_share.wait()
    results = []
    for b in range(2):
        gate = (mod if b == 0 else modx)[5:6, pl.ds(mine, 640)]
        other = precv[256 * (1 - b) : 256 * (2 - b), :]
        total = (own[256 * b : 256 * (b + 1)] + other.astype(F32)).astype(BF).astype(F32)
        before = xt[b, :, :, pl.ds(mine, 640)].reshape(256, 640).astype(F32)
        results.append((before + gate * total).astype(BF).astype(F32))
    cond = jnp.where(c == 0, results[0], results[1])
    uncond = jnp.where(c == 0, results[1], results[0])
    guided = (uncond + GUIDE * (cond - uncond)).astype(BF)
    guided = jnp.where(c == 0, guided[:, 0:HALF], guided[:, 64 : 64 + HALF])
    gs[...] = guided.reshape(PLANE, 16, HALF)

    def back(k, _):
        to = (i + k) % PLANE
        remote(gs.at[to], g2.at[i], r1_s.at[to], r1_r.at[i], on_plane(to)).start()
        return 0

    lax.fori_loop(1, PLANE, back, 0)
    g2[i] = gs[i]

    def take_back(k, _):
        source = (i + PLANE - k) % PLANE
        landed(g2.at[source], r1_r.at[source])
        return 0

    lax.fori_loop(1, PLANE, take_back, 0)
    order = jnp.where(iota((256, 256), 1) == (iota((256, 256), 0) % 64) * 4 + iota((256, 256), 0) // 64, 1.0, 0.0).astype(BF)
    gz[...] = dot(order, g2[...].reshape(256, HALF)).astype(BF).reshape(4, 64, HALF)

    own_block, other_block = [[gz.at[2 * side + f] for f in range(2)] for side in (zh, 1 - zh)]

    def slot(zz):
        return [out.at[f, pl.ds(64 * zz, 64)] for f in range(2)]

    def inner(hh):
        return zh * 4 + hh

    def outer(hh):
        return (1 - zh) * 4 + hh

    out[:, pl.ds(64 * z, 64), :] = gz[pl.ds(2 * zh, 2)]
    for role in range(4):

        @pl.when(h == role)
        def _():
            waits = []

            def go(side, src, zz, index, f, transit=False):
                dst = tr.at[f] if transit else slot(zz)[f]
                recv = r2_r.at[f, RING] if transit else r2_r.at[f, zz]
                remote(src[f], dst, r2_s.at[side, f, index], recv, [left, right][side]).start()
                waits.append((side, f, index))

            def event(side, zz, forward, f):
                landed(slot(zz)[f], r2_r.at[f, zz])
                if forward:
                    go(side, slot(zz), zz, zz, f)

            for f in range(2):
                if role < 2:
                    go(0, other_block, z, RING, f, transit=role == 1)
                else:
                    go(1, other_block, z, RING, f, transit=role == 2)
                if role > 0:
                    go(0, own_block, z, z, f)
                if role < 3:
                    go(1, own_block, z, z, f)
            if role in (0, 3):
                source = inner(1 if role == 0 else 2)
                for f in range(2):
                    landed(tr.at[f], r2_r.at[f, RING])
                    go(0 if role == 0 else 1, [tr.at[0], tr.at[1]], source, source, f)
            lefts = [inner(k) for k in range(role + 1, 4)] + [outer(0), outer(1)]
            rights = [inner(k) for k in range(role - 1, -1, -1)] + [outer(3), outer(2)]
            for k in range(max(len(lefts), len(rights))):
                for f in range(2):
                    if k < len(lefts):
                        event(0, lefts[k], role > 0, f)
                    if k < len(rights):
                        event(1, rights[k], role < 3, f)
            for side, f, index in waits:
                sent(gz.at[0], r2_s.at[side, f, index])

    each_sent(SPACE + TIME, sent_piece)
    lat_out.wait_send()
    sent(lats.at[0], lat_s.at[2])
    for ref, index in pushed:
        sent(ref, wp_s.at[index])
    sent(wsib, wp_s.at[32])

    def done_z(k, _):
        zz = (z + k) % RING
        sent(att.at[zz], za_s.at[zz])
        return 0

    lax.fori_loop(1, RING, done_z, 0)

    def done_plane(k, _):
        ii = (i + k) % PLANE
        sent(xs.at[ii], xy_s.at[ii])
        sent(gs.at[ii], r1_s.at[ii])
        return 0

    lax.fori_loop(1, PLANE, done_plane, 0)

    def done_sibling(k, _):
        sent(xt.at[0, k], sb_s.at[k])
        return 0

    lax.fori_loop(0, PLANE, done_sibling, 0)


def shards(
    latent,
    modulation,
    w_qkv_space,
    w_out_space,
    w_qkv_time,
    w_out_time,
    clip_frames,
    spatial_window,
):
    c = lax.axis_index("cfg")
    lat = latent.reshape(2, POSITIONS, WIDTH)
    wsp = jnp.transpose(w_qkv_space, (1, 2, 0))
    half = lax.dynamic_slice_in_dim(w_qkv_time, c * PAIR, PAIR, 2)
    wt = jnp.concatenate(
        [
            lax.dynamic_slice_in_dim(w_out_space, c * PAIR, PAIR, 0),
            jnp.transpose(half, (1, 2, 0)).reshape(3 * PAIR, WIDTH),
            lax.dynamic_slice_in_dim(w_out_time, c * PAIR, PAIR, 0),
        ],
        axis=0,
    ).reshape(45, GROUP, WIDTH)
    dma = pltpu.SemaphoreType.DMA
    vmem = pl.BlockSpec(memory_space=pltpu.VMEM)
    smem = pl.BlockSpec(memory_space=pltpu.SMEM)
    out = pl.pallas_call(
        kernel,
        out_shape=jax.ShapeDtypeStruct((2, POSITIONS, HALF), BF),
        in_specs=[smem, smem] + [vmem] * 5,
        out_specs=vmem,
        scratch_shapes=[
            pltpu.VMEM((6, WIDTH), F32),
            pltpu.VMEM((2, 384, POSITIONS), BF),
            pltpu.VMEM((2, PAD + POSITIONS + PAD, 384), BF),
            pltpu.VMEM((2, LOCAL, PAD + POSITIONS + PAD), BF),
            pltpu.VMEM((384, 128), F32),
            pltpu.VMEM((RING, LOCAL, 128), BF),
            pltpu.VMEM((WIDTH, 256), BF),
            pltpu.VMEM((2, 16, GROUP, WIDTH), BF),
            pltpu.VMEM((4, LOCAL, WIDTH), BF),
            pltpu.VMEM((4, 64, WIDTH), BF),
            pltpu.VMEM((PLANE, 16, WIDTH), BF),
            pltpu.VMEM((2, PLANE, 16, WIDTH), BF),
            pltpu.VMEM((9, 16, GROUP, WIDTH), BF),
            pltpu.VMEM((256, 256), F32),
            pltpu.VMEM((512, WIDTH), BF),
            pltpu.VMEM((4 * PAIR, 512), BF),
            pltpu.VMEM((512, 640), BF),
            pltpu.VMEM((512, 640), BF),
            pltpu.VMEM((PLANE, 16, HALF), BF),
            pltpu.VMEM((PLANE, 16, HALF), BF),
            pltpu.VMEM((4, 64, HALF), BF),
            pltpu.VMEM((2, 64, HALF), BF),
            dma((2,)),
            dma((4,)),
            dma((9, 3)),
            dma((9,)),
            dma((33,)),
            dma((33,)),
            dma((RING,)),
            dma((RING,)),
            dma((PLANE,)),
            dma((PLANE,)),
            dma((PLANE,)),
            dma((PLANE,)),
            dma((2,)),
            dma((PLANE,)),
            dma((PLANE,)),
            dma((2, 2, RING + 1)),
            dma((2, RING + 1)),
        ],
        compiler_params=pltpu.CompilerParams(
            collective_id=0, has_side_effects=True, vmem_limit_bytes=56 * 1024 * 1024
        ),
        name="sublayers",
    )(spatial_window, clip_frames, lat, modulation[0], wsp, w_out_space, wt)
    return out.reshape(2 * POSITIONS, HALF)


def solution(mesh):
    return jax.shard_map(
        shards,
        mesh=mesh,
        in_specs=(
            P("seq", None),
            P("cfg", None, None),
            P(None, None, "head"),
            P("head", None),
            P(None, None, "head"),
            P("head", None),
            P(),
            P(),
        ),
        out_specs=P("seq", "cfg"),
        check_vma=False,
    )
```

time: 121 us -> 106 us (0.88)
  Pallas kernels: 114 us -> 99.5 us
    pallas_call x1, Pallas kernels: 114 us -> 99.5 us  [shards(): pl.pallas_call(kernel, out_shape=jax.ShapeDtypeStruct((2, POSITIONS, HALF...]
where the time goes in v3:
time: 106 us
  Pallas kernels  99.5 us (94%)
  local copies, waits for them, and re-layouts  4.83 us (5%)
  other arithmetic  1.3 us (1%)
    pallas_call x1, Pallas kernels, shards(): pl.pallas_call(kernel, out_shape=jax.ShapeDtypeStruct((2, POSITIONS, HALF...  99.5 us
    reshape x1, local copies, waits for them, and re-layouts, shards(): return out.reshape(2 * POSITIONS, HALF)  2.38 us

profile of v3, /device:TPU:6, one launch (start us, length us, event | category | flops | bytes accessed | tf_op | source)
XLA Modules:
  0.0 105.6 jit_solution(9456940520626546476)
XLA Ops:
  0.0 0.0 copy-start
  0.0 1.3 %constant_dynamic-slice_fusion = (bf16[144,1152]{1,0:T(8,128)(2,1)S(1)}, bf16[144,1152]{1,0:T(8,128)(2,1)S(1)}) fusion(bf16[288,1152]{1,0:T(8,128)(2,1)} %param.13, s32[]{:T(128)S(6)} %select_n.2, bf16[288,1152]{1,0:T(8,128)(2,1)} %wo.1), kind=kLoop, calls=%fused_computation.2 | loop fusion | bytes 1327108 | tf_op jit(solution)/shard_map/dynamic_slice | solution.py:517
  1.3 0.5 copy-done
  1.8 0.1 constant_dynamic-slice_fusion.1
  1.8 0.0 copy-start.1
  1.8 1.3 %pad_maximum_fusion = bf16[720,1152]{1,0:T(8,128)(2,1)} fusion(bf16[144,1152]{1,0:T(8,128)(2,1)S(1)} %get-tuple-element.5, bf16[432,1152]{1,0:T(8,128)(2,1)S(1)} %bitcast.12, bf16[144,1152]{1,0:T(8,128)(2,1)S(1)} %get-tuple-element.6), kind=kLoop, calls=%fused_computation | loop fusion | flops 4976640 | bytes 3317760 | tf_op jit(solution)/shard_map/concatenate | solution.py:513
  3.1 0.0 copy-done.1
  3.2 0.6 copy.12
  3.8 99.5 %sublayers.1 = bf16[2,512,576]{2,1,0:T(8,128)(2,1)} custom-call(s32[512]{0:T(512)} %sw_ref.1, s32[4]{0:T(128)} %clip_ref.1, bf16[2,512,1152]{2,1,0:T(8,128)(2,1)} %bitcast.13, f32[6,1152]{1,0:T(8,128)} %bitcast.15, bf16[3,288,1152]{2,1,0:T(8,128)(2,1)} %bitcast.14, bf16[288,1152]{1,0:T(8,128)(2,1)} %wo.1, bf16[45,16,1152]{2,1,0:T(8,128)(2,1)} %bitcast.10), custom_call_target="tpu_custom_call" | custom-call | tf_op jit(solution)/shard_map/sublayers/pallas_call | solution.py:524
  103.2 2.4 %copy.9 = bf16[1024,576]{0,1:T(8,128)(2,1)} copy(bf16[1024,576]{1,0:T(8,128)(2,1)} %bitcast.11) | data formatting | bytes 2359296 | tf_op jit(solution)/shard_map/reshape | solution.py:575
Async XLA Ops:
  0.0 1.8 %copy-start = (bf16[1152,3,288]{0,2,1:T(8,128)(2,1)S(1)}, bf16[1152,3,288]{0,2,1:T(8,128)(2,1)}, u32[]{:S(2)}) copy-start(bf16[1152,3,288]{0,2,1:T(8,128)(2,1)} %param.12) | copy-start | bytes 5971972
  1.8 1.3 %copy-start.1 = (f32[1,6,1152]{2,0,1:T(1,128)S(1)}, f32[1,6,1152]{2,0,1:T(1,128)}, u32[]{:S(2)}) copy-start(f32[1,6,1152]{2,0,1:T(1,128)} %param.9) | copy-start | bytes 82948

commit v4 on v3

--- a/solution.py
+++ b/solution.py
@@ -75,9 +75,10 @@
 
 
 def kernel(
-    sw_ref, clip_ref, lat, mod, wsp, wo, wt, out,
-    modx, qt, ks, vt, base, att, heads, wsib, wos, lats, xs, xt, wbuf, tbias, xn, ot, psend, precv, gs, g2, gz, tr,
-    mod_s, lat_s, wz_s, wz_r, wp_s, wp_r, za_s, za_r, xy_s, xy_r, sb_s, sb_r, pp_s, r1_s, r1_r, r2_s, r2_r,
+    sw_ref, clip_ref, lat_in, mod, wsp_in, wo, wqt, wot, out,
+    modx, lat, wsp, wt, qt, ks, vt, base, att, heads, wsib, wos, lats, xs, xt, wbuf, tbias, xn, ot, psend, precv,
+    gs_a, gs_b, g2_a, g2_b, gz_a, gz_b, tr_a, tr_b, land_a, land_b,
+    ld, mod_s, lat_s, wz_s, wz_r, wp_s, wp_r, za_s, za_r, xy_s, xy_r, sb_s, sb_r, pp_s, r1_s, r1_r, r2_s, r2_r,
 ):
     c = lax.axis_index("cfg")
     s = lax.axis_index("seq")
@@ -96,6 +97,25 @@
 
     sib = (1 - c, s, h)
     left, right = on_z((z + RING - 1) % RING), on_z((z + 1) % RING)
+
+    def block_of(zz):
+        return 64 * (2 * (zz % 4) + zz // 4)
+
+    first_rows, last_rows = slice(0, 256), slice(256, 512)
+    loads = [
+        (wo.at[pl.ds(9 * c, 9)], wt.at[0:9]),
+        (lat_in.at[:, first_rows], lat.at[:, first_rows]),
+        (wsp_in, wsp),
+        (wqt.at[0, pl.ds(9 * c, 9)], wt.at[9:18]),
+        (wqt.at[1, pl.ds(9 * c, 9)], wt.at[18:27]),
+        (wqt.at[2, pl.ds(9 * c, 9)], wt.at[27:36]),
+        (wot.at[pl.ds(9 * c, 9)], wt.at[36:45]),
+        (lat_in.at[:, last_rows], lat.at[:, last_rows]),
+        (wo, wos.at[h]),
+    ]
+    loads = [pltpu.make_async_copy(src, dst, ld.at[k]) for k, (src, dst) in enumerate(loads)]
+    for copy in loads:
+        copy.start()
 
     def remote(src, dst, send, recv, dev):
         return pltpu.make_async_remote_copy(
@@ -153,6 +173,7 @@
             there = 16 * (q - first) + place < 3 * per
             pl.when(there)(functools.partial(landed, wbuf.at[q, place], wz_r.at[q]))
 
+    loads[0].wait()
     each_sent(SPACE, start_piece)
 
     pushed = []
@@ -187,7 +208,7 @@
     mod_copy = remote(mod, modx, mod_s.at[0], mod_s.at[1], sib)
     mod_copy.start()
     lat_out = remote(
-        lat.at[c, pl.ds(64 * (7 - z), 64)], lats.at[zh * 2 + c], lat_s.at[0], lat_s.at[1], on_z(7 - z)
+        lat_in.at[c, pl.ds(block_of(7 - z), 64)], lats.at[zh * 2 + c], lat_s.at[0], lat_s.at[1], on_z(7 - z)
     )
     oy = jnp.int32(7)
     ox = jnp.int32(7)
@@ -214,21 +235,20 @@
         vt[f, :, PAD + POSITIONS :] = jnp.zeros((LOCAL, PAD), BF)
         qt[f, LOCAL:384, :] = jnp.zeros((384 - LOCAL, POSITIONS), BF)
 
-    shift1, scale1 = mod[0:1, :], mod[1:2, :]
+    shift1, scale1 = mod[0], mod[1]
     masks = [head_mask(0, 0, 256), head_mask(1, 0, 256), head_mask(2, 0, 256), head_mask(3, 128, 256)]
 
-    for f in range(2):
-        for rb in range(2):
-            rows = slice(rb * 256, (rb + 1) * 256)
+    loads[1].wait()
+    loads[2].wait()
+
+    def project(rb):
+        rows = slice(rb * 256, (rb + 1) * 256)
+        padded = slice(PAD + rb * 256, PAD + (rb + 1) * 256)
+        for f in range(2):
             values = modulated(lat[f, rows, :], shift1, scale1)
             qt[f, 0:LOCAL, rows] = dot_t(wsp[0], values).astype(BF)
-            ks[f, PAD + rb * 256 : PAD + (rb + 1) * 256, 0:LOCAL] = dot_t(values, wsp[1]).astype(BF)
-            vt[f, :, PAD + rb * 256 : PAD + (rb + 1) * 256] = dot_t(wsp[2], values).astype(BF)
-        if f == 0:
-            take_pieces(SPACE)
-            first_phase(0, space_a, space_b)
-            each_sent(TIME, start_piece)
-            lat_out.start()
+            ks[f, padded, 0:LOCAL] = dot_t(values, wsp[1]).astype(BF)
+            vt[f, :, padded] = dot_t(wsp[2], values).astype(BF)
 
     low = iota((1, 128), 1) < 64
 
@@ -251,12 +271,13 @@
         ]
         return jnp.concatenate(parts, axis=0)
 
-    for step in range(2):
-        for k in (2 * step, 2 * step + 1):
-            first, second = attend(k, 0), attend(k, 1)
-            att[2 * k] = jnp.where(low, first, pltpu.roll(second, 64, 1)).astype(BF)
-            att[2 * k + 1] = jnp.where(low, pltpu.roll(first, 64, 1), second).astype(BF)
-        for zd in range(4 * step, 4 * step + 4):
+    def attend_both(k):
+        first, second = attend(k, 0), attend(k, 1)
+        att[k] = jnp.where(low, first, pltpu.roll(second, 64, 1)).astype(BF)
+        att[k + 4] = jnp.where(low, pltpu.roll(first, 64, 1), second).astype(BF)
+
+    def send_heads(k):
+        for zd in (k, k + 4):
             place = heads.at[pl.ds(LOCAL * h, LOCAL), pl.ds(pl.multiple_of(128 * zh, 128), 128)]
             copy = remote(att.at[zd], place, za_s.at[zd], za_r.at[z], on_z(zd))
             pl.when(z != zd)(copy.start)
@@ -265,11 +286,27 @@
             def _():
                 heads[pl.ds(LOCAL * h, LOCAL), pl.ds(pl.multiple_of(128 * zh, 128), 128)] = att[zd]
 
-        if step == 0:
-            first_landed(0, space_a, space_b)
-            second_phase(12, space_a, space_b, (1, 2, 3))
-            take_pieces(TIME)
-            first_phase(6, time_a, time_b)
+    project(0)
+    take_pieces(SPACE)
+    first_phase(0, space_a, space_b)
+    for copy in loads[3:7]:
+        copy.wait()
+    each_sent(TIME, start_piece)
+    lat_out.start()
+    attend_both(0)
+    send_heads(0)
+    loads[7].wait()
+    project(1)
+    first_landed(0, space_a, space_b)
+    second_phase(12, space_a, space_b, (1, 2, 3))
+    attend_both(1)
+    attend_both(2)
+    send_heads(1)
+    send_heads(2)
+    take_pieces(TIME)
+    first_phase(6, time_a, time_b)
+    attend_both(3)
+    send_heads(3)
 
     piece = lats.at[(1 - zh) * 2 + c]
     landed(piece, lat_s.at[1])
@@ -278,15 +315,15 @@
     second_phase(18, time_a, time_b, (1, 3))
     second_landed(12, space_a, space_b, (1, 2, 3))
     remote(wbuf.at[0:2], wsib, wp_s.at[32], wp_r.at[32], sib).start()
-    wos[h] = wo[...]
-    lats[pl.ds(zh * 2, 2)] = lat[:, pl.ds(64 * z, 64), :]
+    loads[8].wait()
+    lats[pl.ds(zh * 2, 2)] = lat[:, pl.ds(block_of(z), 64), :]
     landed(lats.at[(1 - zh) * 2 + (1 - c)], lat_s.at[3])
     landed(wsib, wp_r.at[32])
     for p in range(27):
-        shard, row = (h + 1 + p // 9) % 4, 16 * (p % 9)
+        shard, row = (h + 1 + p // 9) % 4, p % 9
         place = (p // 16, p % 16)
-        wos[shard, pl.ds(PAIR * c + row, 16), :] = wbuf[place]
-        wos[shard, pl.ds(PAIR * (1 - c) + row, 16), :] = wsib[place]
+        wos[shard, 9 * c + row] = wbuf[place]
+        wos[shard, 9 * (1 - c) + row] = wsib[place]
 
     def take_heads(k, _):
         zz = (z + k) % RING
@@ -302,11 +339,11 @@
     for copy in straight:
         copy.start()
 
-    gate1 = mod[2:3, :]
+    gate1 = mod[2]
     order = jnp.where(iota((256, 256), 1) == (iota((256, 256), 0) % 4) * 64 + iota((256, 256), 0) // 4, 1.0, 0.0).astype(BF)
     for n in range(3):
         cols = slice(384 * n, 384 * (n + 1))
-        total = dot_first(heads[...], wos[:, :, cols].reshape(WIDTH, 384))
+        total = dot_first(heads[...], wos[:, :, :, cols].reshape(WIDTH, 384))
         after = lats[:, :, cols].reshape(256, 384).astype(F32) + gate1[:, cols] * total.astype(BF).astype(F32)
         xs[:, :, cols] = dot(order, after.astype(BF)).astype(BF).reshape(PLANE, 16, 384)
 
@@ -332,7 +369,7 @@
         return 0
 
     lax.fori_loop(1, PLANE, pass_on, 0)
-    xn[0:256, :] = modulated(xt[0].reshape(256, WIDTH), mod[3:4, :], mod[4:5, :])
+    xn[0:256, :] = modulated(xt[0].reshape(256, WIDTH), mod[3], mod[4])
 
     def take_sibling(k, _):
         landed(xt.at[1, k], sb_r.at[k])
@@ -340,14 +377,7 @@
 
     lax.fori_loop(0, PLANE, take_sibling, 0)
     mod_copy.wait()
-    xn[256:512, :] = modulated(xt[1].reshape(256, WIDTH), modx[3:4, :], modx[4:5, :])
-
-    landed(wbuf.at[time_a, pl.ds(4 * ((y + 2) % 4), 2)], wp_r.at[24])
-    landed(wbuf.at[time_a, pl.ds(4 * ((y + 2) % 4) + 2, 2)], wp_r.at[25])
-    landed(wbuf.at[time_b, pl.ds(4 * ((x + 2) % 4), 2)], wp_r.at[26])
-    landed(wbuf.at[time_b, pl.ds(4 * ((x + 2) % 4) + 2, 2)], wp_r.at[27])
-    for copy in straight:
-        copy.wait()
+    xn[256:512, :] = modulated(xt[1].reshape(256, WIDTH), modx[3], modx[4])
 
     def groups(slot, first, count):
         if slot == 0:
@@ -356,7 +386,7 @@
         return [wbuf.at[2 + flat // 16, flat % 16] for flat in flats]
 
     pair_masks = [head_mask(n, 0, PAIR) for n in range(2)]
-    for slot in range(4):
+    def time_heads(slot):
         weights = jnp.concatenate([ref[...] for ref in groups(slot, 0, 27)], axis=0)
         three = dot_t(weights, xn[...]).astype(BF)
         for b in range(2):
@@ -372,51 +402,57 @@
             ]
             ot[PAIR * slot : PAIR * (slot + 1), cols] = jnp.concatenate(parts, axis=0).astype(BF)
 
+    time_heads(0)
+    landed(wbuf.at[time_a, pl.ds(4 * ((y + 2) % 4), 2)], wp_r.at[24])
+    landed(wbuf.at[time_a, pl.ds(4 * ((y + 2) % 4) + 2, 2)], wp_r.at[25])
+    landed(wbuf.at[time_b, pl.ds(4 * ((x + 2) % 4), 2)], wp_r.at[26])
+    landed(wbuf.at[time_b, pl.ds(4 * ((x + 2) % 4) + 2, 2)], wp_r.at[27])
+    for copy in straight:
+        copy.wait()
+    for slot in range(1, 4):
+        time_heads(slot)
+
     def share(first):
         refs = [ref for slot in range(4) for ref in groups(slot, 27, 9)]
-        return dot_first(ot[...], jnp.concatenate([ref[:, pl.ds(first, 640)] for ref in refs], axis=0))
-
-    theirs = pl.multiple_of(512 * (1 - c), 128)
-    mine = pl.multiple_of(512 * c, 128)
-    psend[...] = share(theirs).astype(BF)
-    give_share = remote(psend, precv, pp_s.at[0], pp_s.at[1], sib)
-    give_share.start()
-    own = share(mine)
-    give_share.wait()
-    results = []
-    for b in range(2):
-        gate = (mod if b == 0 else modx)[5:6, pl.ds(mine, 640)]
-        other = precv[256 * (1 - b) : 256 * (2 - b), :]
-        total = (own[256 * b : 256 * (b + 1)] + other.astype(F32)).astype(BF).astype(F32)
-        before = xt[b, :, :, pl.ds(mine, 640)].reshape(256, 640).astype(F32)
-        results.append((before + gate * total).astype(BF).astype(F32))
-    cond = jnp.where(c == 0, results[0], results[1])
-    uncond = jnp.where(c == 0, results[1], results[0])
-    guided = (uncond + GUIDE * (cond - uncond)).astype(BF)
-    guided = jnp.where(c == 0, guided[:, 0:HALF], guided[:, 64 : 64 + HALF])
-    gs[...] = guided.reshape(PLANE, 16, HALF)
-
-    def back(k, _):
-        to = (i + k) % PLANE
-        remote(gs.at[to], g2.at[i], r1_s.at[to], r1_r.at[i], on_plane(to)).start()
-        return 0
-
-    lax.fori_loop(1, PLANE, back, 0)
-    g2[i] = gs[i]
-
-    def take_back(k, _):
-        source = (i + PLANE - k) % PLANE
-        landed(g2.at[source], r1_r.at[source])
-        return 0
-
-    lax.fori_loop(1, PLANE, take_back, 0)
-    order = jnp.where(iota((256, 256), 1) == (iota((256, 256), 0) % 64) * 4 + iota((256, 256), 0) // 64, 1.0, 0.0).astype(BF)
-    gz[...] = dot(order, g2[...].reshape(256, HALF)).astype(BF).reshape(4, 64, HALF)
-
-    own_block, other_block = [[gz.at[2 * side + f] for f in range(2)] for side in (zh, 1 - zh)]
-
-    def slot(zz):
-        return [out.at[f, pl.ds(64 * zz, 64)] for f in range(2)]
+        return dot_first(ot[...], jnp.concatenate([ref[:, pl.ds(first, 384)] for ref in refs], axis=0))
+
+    sizes = (256, HALF - 256)
+    gs, g2, gz, tr, land = (gs_a, gs_b), (g2_a, g2_b), (gz_a, gz_b), (tr_a, tr_b), (land_a, land_b)
+
+    def window(core, p):
+        return pl.multiple_of(512 * core + 256 * p, 128)
+
+    give_share = [remote(psend.at[p], precv.at[p], pp_s.at[p], pp_s.at[2 + p], sib) for p in range(2)]
+    for p in range(2):
+        psend[p] = share(window(1 - c, p)).astype(BF)
+        give_share[p].start()
+    for p in range(2):
+        cols = pl.ds(window(c, p), 384)
+        own = share(window(c, p))
+        give_share[p].wait()
+        results = []
+        for b in range(2):
+            gate = (mod if b == 0 else modx)[5, :, cols]
+            other = precv[p, 256 * (1 - b) : 256 * (2 - b), :]
+            total = (own[256 * b : 256 * (b + 1)] + other.astype(F32)).astype(BF).astype(F32)
+            before = xt[b, :, :, cols].reshape(256, 384).astype(F32)
+            results.append((before + gate * total).astype(BF).astype(F32))
+        cond = jnp.where(c == 0, results[0], results[1])
+        uncond = jnp.where(c == 0, results[1], results[0])
+        guided = (uncond + GUIDE * (cond - uncond)).astype(BF)
+        guided = jnp.where(c == 0, guided[:, 0 : sizes[p]], guided[:, 64 : 64 + sizes[p]])
+        gs[p][...] = guided.reshape(PLANE, 16, sizes[p])
+
+        def back(k, _):
+            to = (i + k) % PLANE
+            remote(gs[p].at[to], g2[p].at[i], r1_s.at[p, to], r1_r.at[p, i], on_plane(to)).start()
+            return 0
+
+        lax.fori_loop(1, PLANE, back, 0)
+        g2[p][i] = gs[p][i]
+
+    def slot(zz, p):
+        return land[p].at[zz]
 
     def inner(hh):
         return zh * 4 + hh
@@ -424,48 +460,73 @@
     def outer(hh):
         return (1 - zh) * 4 + hh
 
-    out[:, pl.ds(64 * z, 64), :] = gz[pl.ds(2 * zh, 2)]
+    order = jnp.where(iota((256, 256), 0) == (iota((256, 256), 1) % 64) * 4 + iota((256, 256), 1) // 64, 1.0, 0.0).astype(BF)
+    for p in range(2):
+
+        def take_back(k, _):
+            source = (i + PLANE - k) % PLANE
+            landed(g2[p].at[source], r1_r.at[p, source])
+            return 0
+
+        lax.fori_loop(1, PLANE, take_back, 0)
+        both = dot_first(g2[p][...].reshape(256, sizes[p]), order).astype(BF)
+        gz[p][0] = both[:, 0:128]
+        gz[p][1] = both[:, 128:256]
+        own_block, other_block = gz[p].at[zh], gz[p].at[1 - zh]
+
+        def go(side, src, zz, index, p, transit=False):
+            dst = tr[p] if transit else slot(zz, p)
+            recv = r2_r.at[p, RING] if transit else r2_r.at[p, zz]
+            remote(src, dst, r2_s.at[side, p, index], recv, [left, right][side]).start()
+
+        for role in range(4):
+
+            @pl.when(h == role)
+            def _():
+                go(0 if role < 2 else 1, other_block, z, RING, p, transit=role in (1, 2))
+                if role > 0:
+                    go(0, own_block, z, z, p)
+                if role < 3:
+                    go(1, own_block, z, z, p)
+
+        land[p][z] = gz[p][zh]
+
     for role in range(4):
 
         @pl.when(h == role)
         def _():
             waits = []
-
-            def go(side, src, zz, index, f, transit=False):
-                dst = tr.at[f] if transit else slot(zz)[f]
-                recv = r2_r.at[f, RING] if transit else r2_r.at[f, zz]
-                remote(src[f], dst, r2_s.at[side, f, index], recv, [left, right][side]).start()
-                waits.append((side, f, index))
-
-            def event(side, zz, forward, f):
-                landed(slot(zz)[f], r2_r.at[f, zz])
-                if forward:
-                    go(side, slot(zz), zz, zz, f)
-
-            for f in range(2):
-                if role < 2:
-                    go(0, other_block, z, RING, f, transit=role == 1)
-                else:
-                    go(1, other_block, z, RING, f, transit=role == 2)
-                if role > 0:
-                    go(0, own_block, z, z, f)
-                if role < 3:
-                    go(1, own_block, z, z, f)
             if role in (0, 3):
                 source = inner(1 if role == 0 else 2)
-                for f in range(2):
-                    landed(tr.at[f], r2_r.at[f, RING])
-                    go(0 if role == 0 else 1, [tr.at[0], tr.at[1]], source, source, f)
+                for p in range(2):
+                    landed(tr[p], r2_r.at[p, RING])
+                    go(0 if role == 0 else 1, tr[p], source, source, p)
+                    waits.append((0 if role == 0 else 1, source, p))
             lefts = [inner(k) for k in range(role + 1, 4)] + [outer(0), outer(1)]
             rights = [inner(k) for k in range(role - 1, -1, -1)] + [outer(3), outer(2)]
             for k in range(max(len(lefts), len(rights))):
-                for f in range(2):
-                    if k < len(lefts):
-                        event(0, lefts[k], role > 0, f)
-                    if k < len(rights):
-                        event(1, rights[k], role < 3, f)
-            for side, f, index in waits:
-                sent(gz.at[0], r2_s.at[side, f, index])
+                for p in range(2):
+                    for side, chain, forward in ((0, lefts, role > 0), (1, rights, role < 3)):
+                        if k < len(chain):
+                            landed(slot(chain[k], p), r2_r.at[p, chain[k]])
+                            if forward:
+                                go(side, slot(chain[k], p), chain[k], chain[k], p)
+                                waits.append((side, chain[k], p))
+            for p in range(2):
+                waits.append((0 if role < 2 else 1, RING, p))
+                if role > 0:
+                    waits.append((0, z, p))
+                if role < 3:
+                    waits.append((1, z, p))
+            for side, index, p in waits:
+                sent(tr[p], r2_s.at[side, p, index])
+
+    for p in range(2):
+        rows = slice(256 * p, 256 * p + sizes[p])
+        for k in range(4):
+            first, second = land[p][k].astype(F32), land[p][k + 4].astype(F32)
+            out[rows, 128 * k : 128 * (k + 1)] = jnp.where(low, first, pltpu.roll(second, 64, 1)).astype(BF)
+            out[rows, 512 + 128 * k : 512 + 128 * (k + 1)] = jnp.where(low, pltpu.roll(first, 64, 1), second).astype(BF)
 
     each_sent(SPACE + TIME, sent_piece)
     lat_out.wait_send()
@@ -484,7 +545,8 @@
     def done_plane(k, _):
         ii = (i + k) % PLANE
         sent(xs.at[ii], xy_s.at[ii])
-        sent(gs.at[ii], r1_s.at[ii])
+        for p in range(2):
+            sent(gs[p].at[ii], r1_s.at[p, ii])
         return 0
 
     lax.fori_loop(1, PLANE, done_plane, 0)
@@ -506,28 +568,25 @@
     clip_frames,
     spatial_window,
 ):
-    c = lax.axis_index("cfg")
     lat = latent.reshape(2, POSITIONS, WIDTH)
     wsp = jnp.transpose(w_qkv_space, (1, 2, 0))
-    half = lax.dynamic_slice_in_dim(w_qkv_time, c * PAIR, PAIR, 2)
-    wt = jnp.concatenate(
-        [
-            lax.dynamic_slice_in_dim(w_out_space, c * PAIR, PAIR, 0),
-            jnp.transpose(half, (1, 2, 0)).reshape(3 * PAIR, WIDTH),
-            lax.dynamic_slice_in_dim(w_out_time, c * PAIR, PAIR, 0),
-        ],
-        axis=0,
-    ).reshape(45, GROUP, WIDTH)
+    wqt = jnp.transpose(w_qkv_time, (1, 2, 0)).reshape(3, 18, GROUP, WIDTH)
+    wo = w_out_space.reshape(18, GROUP, WIDTH)
+    wot = w_out_time.reshape(18, GROUP, WIDTH)
     dma = pltpu.SemaphoreType.DMA
     vmem = pl.BlockSpec(memory_space=pltpu.VMEM)
     smem = pl.BlockSpec(memory_space=pltpu.SMEM)
+    anywhere = pl.BlockSpec(memory_space=pl.ANY)
     out = pl.pallas_call(
         kernel,
-        out_shape=jax.ShapeDtypeStruct((2, POSITIONS, HALF), BF),
-        in_specs=[smem, smem] + [vmem] * 5,
+        out_shape=jax.ShapeDtypeStruct((HALF, 2 * POSITIONS), BF),
+        in_specs=[smem, smem, anywhere, vmem] + [anywhere] * 4,
         out_specs=vmem,
         scratch_shapes=[
-            pltpu.VMEM((6, WIDTH), F32),
+            pltpu.VMEM((6, 1, WIDTH), F32),
+            pltpu.VMEM((2, POSITIONS, WIDTH), BF),
+            pltpu.VMEM((3, LOCAL, WIDTH), BF),
+            pltpu.VMEM((45, GROUP, WIDTH), BF),
             pltpu.VMEM((2, 384, POSITIONS), BF),
             pltpu.VMEM((2, PAD + POSITIONS + PAD, 384), BF),
             pltpu.VMEM((2, LOCAL, PAD + POSITIONS + PAD), BF),
@@ -535,7 +594,7 @@
             pltpu.VMEM((RING, LOCAL, 128), BF),
             pltpu.VMEM((WIDTH, 256), BF),
             pltpu.VMEM((2, 16, GROUP, WIDTH), BF),
-            pltpu.VMEM((4, LOCAL, WIDTH), BF),
+            pltpu.VMEM((4, 18, GROUP, WIDTH), BF),
             pltpu.VMEM((4, 64, WIDTH), BF),
             pltpu.VMEM((PLANE, 16, WIDTH), BF),
             pltpu.VMEM((2, PLANE, 16, WIDTH), BF),
@@ -543,12 +602,19 @@
             pltpu.VMEM((256, 256), F32),
             pltpu.VMEM((512, WIDTH), BF),
             pltpu.VMEM((4 * PAIR, 512), BF),
-            pltpu.VMEM((512, 640), BF),
-            pltpu.VMEM((512, 640), BF),
-            pltpu.VMEM((PLANE, 16, HALF), BF),
-            pltpu.VMEM((PLANE, 16, HALF), BF),
-            pltpu.VMEM((4, 64, HALF), BF),
-            pltpu.VMEM((2, 64, HALF), BF),
+            pltpu.VMEM((2, 512, 384), BF),
+            pltpu.VMEM((2, 512, 384), BF),
+            pltpu.VMEM((PLANE, 16, 256), BF),
+            pltpu.VMEM((PLANE, 16, HALF - 256), BF),
+            pltpu.VMEM((PLANE, 16, 256), BF),
+            pltpu.VMEM((PLANE, 16, HALF - 256), BF),
+            pltpu.VMEM((2, 256, 128), BF),
+            pltpu.VMEM((2, HALF - 256, 128), BF),
+            pltpu.VMEM((256, 128), BF),
+            pltpu.VMEM((HALF - 256, 128), BF),
+            pltpu.VMEM((RING, 256, 128), BF),
+            pltpu.VMEM((RING, HALF - 256, 128), BF),
+            dma((9,)),
             dma((2,)),
             dma((4,)),
             dma((9, 3)),
@@ -561,9 +627,9 @@
             dma((PLANE,)),
             dma((PLANE,)),
             dma((PLANE,)),
-            dma((2,)),
-            dma((PLANE,)),
-            dma((PLANE,)),
+            dma((4,)),
+            dma((2, PLANE)),
+            dma((2, PLANE)),
             dma((2, 2, RING + 1)),
             dma((2, RING + 1)),
         ],
@@ -571,8 +637,8 @@
             collective_id=0, has_side_effects=True, vmem_limit_bytes=56 * 1024 * 1024
         ),
         name="sublayers",
-    )(spatial_window, clip_frames, lat, modulation[0], wsp, w_out_space, wt)
-    return out.reshape(2 * POSITIONS, HALF)
+    )(spatial_window, clip_frames, lat, jnp.transpose(modulation, (1, 0, 2)), wsp, wo, wqt, wot)
+    return jnp.transpose(out)
 
 
 def solution(mesh):

time: 106 us -> 95.2 us (0.90)
  Pallas kernels: 99.5 us -> 91.6 us
  local copies, waits for them, and re-layouts: 4.83 us -> 2.36 us
  other arithmetic: 1.3 us -> 0 us
    pallas_call x1, Pallas kernels: 99.5 us -> 91.6 us  [shards(): pl.pallas_call(kernel, out_shape=jax.ShapeDtypeStruct((HALF, 2 * POSITION...]
    reshape x1 -> x0, local copies, waits for them, and re-layouts: 2.38 us -> none  [shards(): return out.reshape(2 * POSITIONS, HALF)]
    dynamic_slice x2 -> x0, local copies, waits for them, and re-layouts: 1.35 us -> none  [the longest x1 1.27 us: shards(): lax.dynamic_slice_in_dim(w_out_time, c * PAIR, PAIR, 0)]
    concatenate x1 -> x0, other arithmetic: 1.3 us -> none  [shards(): jnp.concatenate([lax.dynamic_slice_in_dim(w_out_space, c * PAIR, PAIR, 0)...]
    unnamed x5 -> x1, local copies, waits for them, and re-layouts: 1.11 us -> 2.36 us
where the time goes in v4:
time: 95.2 us; the launch traced here: 94 us
  Pallas kernels  91.6 us (96%)
  local copies, waits for them, and re-layouts  2.36 us (2%)
    pallas_call x1, Pallas kernels, shards(): pl.pallas_call(kernel, out_shape=jax.ShapeDtypeStruct((HALF, 2 * POSITION...  91.6 us
    unnamed x1, local copies, waits for them, and re-layouts  2.36 us

profile of v4, /device:TPU:6, one launch (start us, length us, event | category | flops | bytes accessed | tf_op | source)
XLA Modules:
  0.0 94.0 jit_solution(10774259921320015411)
XLA Ops:
  0.0 91.6 %sublayers.1 = bf16[576,1024]{1,0:T(8,128)(2,1)} custom-call(s32[512]{0:T(512)} %sw_ref.1, s32[4]{0:T(128)} %clip_ref.1, bf16[2,512,1152]{2,1,0:T(8,128)(2,1)} %bitcast.10, f32[6,1,1152]{2,1,0:T(1,128)} %bitcast.15, bf16[3,288,1152]{2,1,0:T(8,128)(2,1)} %bitcast.11, bf16[18,16,1152]{2,1,0:T(8,128)(2,1)} %bitcast.13, bf16[3,18,16,1152]{3,2,1,0:T(8,128)(2,1)} %bitcast.12, ...), custom_call_target="tpu_custom_call" | custom-call | tf_op jit(solution)/shard_map/sublayers/pallas_call | solution.py:580
  91.6 2.4 %copy.10 = bf16[1024,576]{0,1:T(8,128)(2,1)} copy(bf16[1024,576]{0,1:T(8,128)(2,1)} %bitcast.9) | data formatting | bytes 2359296

commit v5 on v4

--- a/solution.py
+++ b/solution.py
@@ -75,7 +75,7 @@
 
 
 def kernel(
-    sw_ref, clip_ref, lat_in, mod, wsp_in, wo, wqt, wot, out,
+    sw_ref, clip_ref, lat_in, mod, wsp_in, wo, wqt, wot, out_a, out_b,
     modx, lat, wsp, wt, qt, ks, vt, base, att, heads, wsib, wos, lats, xs, xt, wbuf, tbias, xn, ot, psend, precv,
     gs_a, gs_b, g2_a, g2_b, gz_a, gz_b, tr_a, tr_b, land_a, land_b,
     ld, mod_s, lat_s, wz_s, wz_r, wp_s, wp_r, za_s, za_r, xy_s, xy_r, sb_s, sb_r, pp_s, r1_s, r1_r, r2_s, r2_r,
@@ -220,13 +220,6 @@
     same = ((qj // 16 + 8 + oy) // 8 == (ki // 16 + oy) // 8) & ((qj % 16 + ox) // 8 == (ki % 16 + ox) // 8)
     base[...] = jnp.where(same, 0.0, NEG)
 
-    def time_key(row):
-        four = row % 4
-        frame = (four // 2) * 32 + 2 * (row // 16) + four % 2
-        return frame_window(frame, clip_ref) * 4 + (row % 16) // 4
-
-    tbias[...] = jnp.where(time_key(iota((256, 1), 0)) == time_key(iota((1, 256), 1)), 0.0, NEG)
-
     for f in range(2):
         ks[f, 0:PAD, :] = jnp.zeros((PAD, 384), BF)
         ks[f, PAD + POSITIONS :, :] = jnp.zeros((PAD, 384), BF)
@@ -241,14 +234,13 @@
     loads[1].wait()
     loads[2].wait()
 
-    def project(rb):
+    def project(rb, f):
         rows = slice(rb * 256, (rb + 1) * 256)
         padded = slice(PAD + rb * 256, PAD + (rb + 1) * 256)
-        for f in range(2):
-            values = modulated(lat[f, rows, :], shift1, scale1)
-            qt[f, 0:LOCAL, rows] = dot_t(wsp[0], values).astype(BF)
-            ks[f, padded, 0:LOCAL] = dot_t(values, wsp[1]).astype(BF)
-            vt[f, :, padded] = dot_t(wsp[2], values).astype(BF)
+        values = modulated(lat[f, rows, :], shift1, scale1)
+        qt[f, 0:LOCAL, rows] = dot_t(wsp[0], values).astype(BF)
+        ks[f, padded, 0:LOCAL] = dot_t(values, wsp[1]).astype(BF)
+        vt[f, :, padded] = dot_t(wsp[2], values).astype(BF)
 
     low = iota((1, 128), 1) < 64
 
@@ -286,27 +278,33 @@
             def _():
                 heads[pl.ds(LOCAL * h, LOCAL), pl.ds(pl.multiple_of(128 * zh, 128), 128)] = att[zd]
 
-    project(0)
-    take_pieces(SPACE)
-    first_phase(0, space_a, space_b)
     for copy in loads[3:7]:
         copy.wait()
     each_sent(TIME, start_piece)
     lat_out.start()
+    project(0, 0)
+    take_pieces(SPACE)
+    first_phase(0, space_a, space_b)
+    project(0, 1)
     attend_both(0)
     send_heads(0)
-    loads[7].wait()
-    project(1)
     first_landed(0, space_a, space_b)
     second_phase(12, space_a, space_b, (1, 2, 3))
-    attend_both(1)
-    attend_both(2)
-    send_heads(1)
-    send_heads(2)
     take_pieces(TIME)
     first_phase(6, time_a, time_b)
-    attend_both(3)
-    send_heads(3)
+    loads[7].wait()
+    project(1, 0)
+    project(1, 1)
+    for k in range(1, 4):
+        attend_both(k)
+        send_heads(k)
+
+    def time_key(row):
+        four = row % 4
+        frame = (four // 2) * 32 + 2 * (row // 16) + four % 2
+        return frame_window(frame, clip_ref) * 4 + (row % 16) // 4
+
+    tbias[...] = jnp.where(time_key(iota((256, 1), 0)) == time_key(iota((1, 256), 1)), 0.0, NEG)
 
     piece = lats.at[(1 - zh) * 2 + c]
     landed(piece, lat_s.at[1])
@@ -361,23 +359,37 @@
     xt[0, i] = xs[i]
     remote(xs.at[i], xt.at[1, i], sb_s.at[i], sb_r.at[i], sib).start()
 
-    def pass_on(k, _):
-        source = (i + PLANE - k) % PLANE
-        piece = xt.at[0, source]
-        landed(piece, xy_r.at[source])
-        remote(piece, xt.at[1, source], sb_s.at[source], sb_r.at[source], sib).start()
-        return 0
-
-    lax.fori_loop(1, PLANE, pass_on, 0)
-    xn[0:256, :] = modulated(xt[0].reshape(256, WIDTH), mod[3], mod[4])
-
-    def take_sibling(k, _):
-        landed(xt.at[1, k], sb_r.at[k])
-        return 0
-
-    lax.fori_loop(0, PLANE, take_sibling, 0)
     mod_copy.wait()
-    xn[256:512, :] = modulated(xt[1].reshape(256, WIDTH), modx[3], modx[4])
+
+    def own_group(n):
+        g = (i // 4 + 4 - n) % 4
+        for m in range(4):
+            source = 4 * g + m
+
+            @pl.when(source != i)
+            def _():
+                piece = xt.at[0, source]
+                landed(piece, xy_r.at[source])
+                remote(piece, xt.at[1, source], sb_s.at[source], sb_r.at[source], sib).start()
+
+        rows = xt[0, pl.ds(4 * g, 4)].reshape(64, WIDTH)
+        xn[pl.ds(64 * g, 64), :] = modulated(rows, mod[3], mod[4])
+
+    def sibling_group(n):
+        g = (i // 4 + 4 - n) % 4
+        for m in range(4):
+            landed(xt.at[1, 4 * g + m], sb_r.at[4 * g + m])
+        rows = xt[1, pl.ds(4 * g, 4)].reshape(64, WIDTH)
+        xn[pl.ds(256 + 64 * g, 64), :] = modulated(rows, modx[3], modx[4])
+
+    own_group(0)
+    own_group(1)
+    sibling_group(0)
+    own_group(2)
+    sibling_group(1)
+    own_group(3)
+    sibling_group(2)
+    sibling_group(3)
 
     def groups(slot, first, count):
         if slot == 0:
@@ -522,11 +534,11 @@
                 sent(tr[p], r2_s.at[side, p, index])
 
     for p in range(2):
-        rows = slice(256 * p, 256 * p + sizes[p])
+        out = (out_a, out_b)[p]
         for k in range(4):
             first, second = land[p][k].astype(F32), land[p][k + 4].astype(F32)
-            out[rows, 128 * k : 128 * (k + 1)] = jnp.where(low, first, pltpu.roll(second, 64, 1)).astype(BF)
-            out[rows, 512 + 128 * k : 512 + 128 * (k + 1)] = jnp.where(low, pltpu.roll(first, 64, 1), second).astype(BF)
+            out[:, 128 * k : 128 * (k + 1)] = jnp.where(low, first, pltpu.roll(second, 64, 1)).astype(BF)
+            out[:, 512 + 128 * k : 512 + 128 * (k + 1)] = jnp.where(low, pltpu.roll(first, 64, 1), second).astype(BF)
 
     each_sent(SPACE + TIME, sent_piece)
     lat_out.wait_send()
@@ -577,11 +589,11 @@
     vmem = pl.BlockSpec(memory_space=pltpu.VMEM)
     smem = pl.BlockSpec(memory_space=pltpu.SMEM)
     anywhere = pl.BlockSpec(memory_space=pl.ANY)
-    out = pl.pallas_call(
+    out_a, out_b = pl.pallas_call(
         kernel,
-        out_shape=jax.ShapeDtypeStruct((HALF, 2 * POSITIONS), BF),
+        out_shape=[jax.ShapeDtypeStruct((rows, 2 * POSITIONS), BF) for rows in (256, HALF - 256)],
         in_specs=[smem, smem, anywhere, vmem] + [anywhere] * 4,
-        out_specs=vmem,
+        out_specs=[vmem, vmem],
         scratch_shapes=[
             pltpu.VMEM((6, 1, WIDTH), F32),
             pltpu.VMEM((2, POSITIONS, WIDTH), BF),
@@ -638,7 +650,7 @@
         ),
         name="sublayers",
     )(spatial_window, clip_frames, lat, jnp.transpose(modulation, (1, 0, 2)), wsp, wo, wqt, wot)
-    return jnp.transpose(out)
+    return jnp.transpose(jnp.concatenate([out_a, out_b], axis=0))
 
 
 def solution(mesh):

time: 95.2 us -> 95.5 us (level); the launches traced: 94 us -> 95.4 us
  local copies, waits for them, and re-layouts: 2.36 us -> 0 us
  other arithmetic: 0 us -> 2.33 us
  Pallas kernels: 91.6 us -> 93 us
    unnamed x1 -> x0, local copies, waits for them, and re-layouts: 2.36 us -> none
    transpose x0 -> x1, other arithmetic: none -> 2.33 us  [shards(): return jnp.transpose(jnp.concatenate([out_a, out_b], axis=0))]
    pallas_call x1, Pallas kernels: 91.6 us -> 93 us  [shards(): pl.pallas_call(kernel, out_shape=[jax.ShapeDtypeStruct((rows, 2 * POSITIO...]
where the time goes in v5:
time: 95.5 us; the launch traced here: 95.4 us
  Pallas kernels  93 us (97%)
  other arithmetic  2.33 us (2%)
    pallas_call x1, Pallas kernels, shards(): pl.pallas_call(kernel, out_shape=[jax.ShapeDtypeStruct((rows, 2 * POSITIO...  93 us
    transpose x1, other arithmetic, shards(): return jnp.transpose(jnp.concatenate([out_a, out_b], axis=0))  2.33 us

profile of v5, /device:TPU:6, one launch (start us, length us, event | category | flops | bytes accessed | tf_op | source)
XLA Modules:
  0.0 95.4 jit_solution(9965686988040207565)
XLA Ops:
  0.0 93.0 %sublayers.1 = (bf16[256,1024]{1,0:T(8,128)(2,1)}, bf16[320,1024]{1,0:T(8,128)(2,1)}) custom-call(s32[512]{0:T(512)} %sw_ref.1, s32[4]{0:T(128)} %clip_ref.1, bf16[2,512,1152]{2,1,0:T(8,128)(2,1)} %bitcast.10, f32[6,1,1152]{2,1,0:T(1,128)} %bitcast.15, bf16[3,288,1152]{2,1,0:T(8,128)(2,1)} %bitcast.11, bf16[18,16,1152]{2,1,0:T(8,128)(2,1)} %bitcast.13, ...), custom_call_target="tpu_custom_call" | custom-call | tf_op jit(solution)/shard_map/sublayers/pallas_call | solution.py:592
  93.0 2.3 %maximum_bitcast_fusion = bf16[1024,576]{0,1:T(8,128)(2,1)} fusion(bf16[320,1024]{1,0:T(8,128)(2,1)} %get-tuple-element.8, bf16[256,1024]{1,0:T(8,128)(2,1)} %get-tuple-element.7), kind=kLoop, calls=%fused_computation | loop fusion | flops 2359296 | bytes 2359296 | tf_op jit(solution)/shard_map/transpose | solution.py:653

commit v6 on v5

--- a/solution.py
+++ b/solution.py
@@ -76,7 +76,7 @@
 
 def kernel(
     sw_ref, clip_ref, lat_in, mod, wsp_in, wo, wqt, wot, out_a, out_b,
-    modx, lat, wsp, wt, qt, ks, vt, base, att, heads, wsib, wos, lats, xs, xt, wbuf, tbias, xn, ot, psend, precv,
+    modx, lat, wsp, wt, qt, ks, vt, base, att, heads, wsib, wos, lats, xs, xt, wbuf, tbias, xn, ot, xh, psend, precv,
     gs_a, gs_b, g2_a, g2_b, gz_a, gz_b, tr_a, tr_b, land_a, land_b,
     ld, mod_s, lat_s, wz_s, wz_r, wp_s, wp_r, za_s, za_r, xy_s, xy_r, sb_s, sb_r, pp_s, r1_s, r1_r, r2_s, r2_r,
 ):
@@ -424,9 +424,10 @@
     for slot in range(1, 4):
         time_heads(slot)
 
+    xh[...] = jnp.transpose(ot[...])
     def share(first):
         refs = [ref for slot in range(4) for ref in groups(slot, 27, 9)]
-        return dot_first(ot[...], jnp.concatenate([ref[:, pl.ds(first, 384)] for ref in refs], axis=0))
+        return dot(xh[...], jnp.concatenate([ref[:, pl.ds(first, 384)] for ref in refs], axis=0))
 
     sizes = (256, HALF - 256)
     gs, g2, gz, tr, land = (gs_a, gs_b), (g2_a, g2_b), (gz_a, gz_b), (tr_a, tr_b), (land_a, land_b)
@@ -591,7 +592,7 @@
     anywhere = pl.BlockSpec(memory_space=pl.ANY)
     out_a, out_b = pl.pallas_call(
         kernel,
-        out_shape=[jax.ShapeDtypeStruct((rows, 2 * POSITIONS), BF) for rows in (256, HALF - 256)],
+        out_shape=[pltpu.VMEM((rows, 2 * POSITIONS), BF) for rows in (256, HALF - 256)],
         in_specs=[smem, smem, anywhere, vmem] + [anywhere] * 4,
         out_specs=[vmem, vmem],
         scratch_shapes=[
@@ -614,6 +615,7 @@
             pltpu.VMEM((256, 256), F32),
             pltpu.VMEM((512, WIDTH), BF),
             pltpu.VMEM((4 * PAIR, 512), BF),
+            pltpu.VMEM((512, 4 * PAIR), BF),
             pltpu.VMEM((2, 512, 384), BF),
             pltpu.VMEM((2, 512, 384), BF),
             pltpu.VMEM((PLANE, 16, 256), BF),

time: 95.5 us -> 93.2 us (0.976)
  Pallas kernels: 93 us -> 91.7 us
  other arithmetic: 2.33 us -> 1.1 us
    pallas_call x1, Pallas kernels: 93 us -> 91.7 us  [shards(): pl.pallas_call(kernel, out_shape=[pltpu.VMEM((rows, 2 * POSITIONS), BF) f...]
    transpose x1, other arithmetic: 2.33 us -> 1.1 us  [shards(): return jnp.transpose(jnp.concatenate([out_a, out_b], axis=0))]
where the time goes in v6:
time: 93.2 us; the launch traced here: 92.8 us
  Pallas kernels  91.7 us (98%)
  other arithmetic  1.1 us (1%)
    pallas_call x1, Pallas kernels, shards(): pl.pallas_call(kernel, out_shape=[pltpu.VMEM((rows, 2 * POSITIONS), BF) f...  91.7 us

profile of v6, /device:TPU:6, one launch (start us, length us, event | category | flops | bytes accessed | tf_op | source)
XLA Modules:
  0.0 92.8 jit_solution(3625764514090556797)
XLA Ops:
  0.0 91.7 %sublayers.1 = (bf16[256,1024]{1,0:T(8,128)(2,1)S(1)}, bf16[320,1024]{1,0:T(8,128)(2,1)S(1)}) custom-call(s32[512]{0:T(512)} %sw_ref.1, s32[4]{0:T(128)} %clip_ref.1, bf16[2,512,1152]{2,1,0:T(8,128)(2,1)} %bitcast.10, f32[6,1,1152]{2,1,0:T(1,128)} %bitcast.15, bf16[3,288,1152]{2,1,0:T(8,128)(2,1)} %bitcast.11, bf16[18,16,1152]{2,1,0:T(8,128)(2,1)} %bitcast.13, ...), custom_call_target="tpu_custom_call" | custom-call | tf_op jit(solution)/shard_map/sublayers/pallas_call | solution.py:593
  91.7 1.1 %maximum_bitcast_fusion = bf16[1024,576]{0,1:T(8,128)(2,1)} fusion(bf16[320,1024]{1,0:T(8,128)(2,1)S(1)} %get-tuple-element.8, bf16[256,1024]{1,0:T(8,128)(2,1)S(1)} %get-tuple-element.7), kind=kLoop, calls=%fused_computation | loop fusion | flops 2359296 | bytes 2359296 | tf_op jit(solution)/shard_map/transpose | solution.py:655

commit v7 on v6

--- a/solution.py
+++ b/solution.py
@@ -36,7 +36,7 @@
     centred = values - jnp.mean(values, axis=-1, keepdims=True)
     spread = jnp.mean(centred * centred, axis=-1, keepdims=True)
     normed = centred * lax.rsqrt(spread + EPSILON)
-    return (normed * (1.0 + scale) + shift).astype(BF)
+    return (normed * (1.0 + shift * 0.0 + scale) + shift).astype(BF)
 
 
 def softmax_keys(scores):

time: 93.2 us -> 93.1 us (level)
  no operation moved by 1% of the time
where the time goes in v7:
time: 93.1 us; the launch traced here: 92.7 us
  Pallas kernels  91.6 us (98%)
  other arithmetic  1.1 us (1%)
    pallas_call x1, Pallas kernels, shards(): pl.pallas_call(kernel, out_shape=[pltpu.VMEM((rows, 2 * POSITIONS), BF) f...  91.6 us

profile of v7, /device:TPU:6, one launch (start us, length us, event | category | flops | bytes accessed | tf_op | source)
XLA Modules:
  0.0 92.7 jit_solution(1326756332954792526)
XLA Ops:
  0.0 91.6 %sublayers.1 = (bf16[256,1024]{1,0:T(8,128)(2,1)S(1)}, bf16[320,1024]{1,0:T(8,128)(2,1)S(1)}) custom-call(s32[512]{0:T(512)} %sw_ref.1, s32[4]{0:T(128)} %clip_ref.1, bf16[2,512,1152]{2,1,0:T(8,128)(2,1)} %bitcast.10, f32[6,1,1152]{2,1,0:T(1,128)} %bitcast.15, bf16[3,288,1152]{2,1,0:T(8,128)(2,1)} %bitcast.11, bf16[18,16,1152]{2,1,0:T(8,128)(2,1)} %bitcast.13, ...), custom_call_target="tpu_custom_call" | custom-call | tf_op jit(solution)/shard_map/sublayers/pallas_call | solution.py:593
  91.6 1.1 %maximum_bitcast_fusion = bf16[1024,576]{0,1:T(8,128)(2,1)} fusion(bf16[320,1024]{1,0:T(8,128)(2,1)S(1)} %get-tuple-element.8, bf16[256,1024]{1,0:T(8,128)(2,1)S(1)} %get-tuple-element.7), kind=kLoop, calls=%fused_computation | loop fusion | flops 2359296 | bytes 2359296 | tf_op jit(solution)/shard_map/transpose | solution.py:655
